TPU v7x, 256 devices: a whole 4x4x8 slice. The times are simulated.
256 devices in a mesh: pipe: 8 (over y, x_hi), expert: 32 (over x_lo, z, core).
Axes of the slice: x: 4 (x_hi: 2, x_lo: 2; x = x_hi * 2 + x_lo), y: 4, z: 8, core: 2. Of those that a mesh axis runs over, the one named last changes fastest.
Arguments:
- fwd_state: bfloat16 [8, 1024, 3584], P('pipe', 'expert'), may hold values from -6 to 6
- new_tokens: bfloat16 [1, 1024, 3584], P(None, 'expert'), may hold values from -6 to 6
- saved_input: bfloat16 [2, 8, 1024, 3584], P(None, 'pipe', 'expert'), may hold values from -6 to 6
- grad_state: bfloat16 [8, 1024, 3584], P('pipe', 'expert'), may hold values from -6 to 6
- new_grads: bfloat16 [1, 1024, 3584], P(None, 'expert'), may hold values from -6 to 6
- norm_gain: float32 [8, 3584], P('pipe'), may hold values from 0.25 to 1.75
- w_gate: bfloat16 [8, 3584, 16384], P('pipe', None, 'expert'), may hold values from -0.09375 to 0.09375
- w_up: bfloat16 [8, 3584, 16384], P('pipe', None, 'expert'), may hold values from -0.09375 to 0.09375
- w_down: bfloat16 [8, 16384, 3584], P('pipe', 'expert'), may hold values from -0.1875 to 0.1875
- fwd_ids: int32 [2, 8, 1024, 4], P(None, 'pipe', 'expert'), may hold values from 0 to 15, all different within a row; in each aligned block of 32 rows (0 to 31, 32 to 63, ..., all dimensions but the last counted through in order) at most 8 rows name the same one
- fwd_gates: float32 [2, 8, 1024, 4], P(None, 'pipe', 'expert'), may hold values from 0.05 to 0.6
- bwd_ids: int32 [2, 8, 1024, 4], P(None, 'pipe', 'expert'), may hold values from 0 to 15, all different within a row; in each aligned block of 32 rows (0 to 31, 32 to 63, ..., all dimensions but the last counted through in order) at most 8 rows name the same one
- bwd_gates: float32 [2, 8, 1024, 4], P(None, 'pipe', 'expert'), may hold values from 0.05 to 0.6
Outputs:
- fwd_out: bfloat16 [8, 1024, 3584], P('pipe', 'expert')
- grad_out: bfloat16 [8, 1024, 3584], P('pipe', 'expert')
Inputs may be any that keep to these rules, and one draw needn't show every extreme that they name: `fwd_ids`: each row names 4 different experts. In every aligned block of 32 rows (the tokens of one index of expert for one tick and layer) every expert is named by exactly 8 rows. `bwd_ids`: as for fwd_ids.
All inputs are finite; a program needn't handle non-finite values.
Results may differ from a plain program's by a relative error of at most 0.01.
Values may be sent and summed in bfloat16 or wider, within the bound.
A program may use at most 64 MiB of HBM per device.

v0:
```python
import jax
import jax.numpy as jnp
from jax import lax
from jax.sharding import PartitionSpec as P


def shifted(value, axis, steps):
    count = lax.axis_size(axis)
    first, last = (max(0, -steps), min(count, count - steps))
    return lax.ppermute(value, axis, [(source, source + steps) for source in range(first, last)])


def normalize(activations, gain_row):
    widened = activations.astype(jnp.float32)
    inverse_rms = lax.rsqrt(jnp.mean(widened * widened, axis=-1, keepdims=True) + 1e-06)
    normed = (widened * inverse_rms * gain_row).astype(jnp.bfloat16)
    return (normed, widened, inverse_rms)


def route_slots(route_ids, capacity, expert_count):
    count_rows = route_ids.shape[0] * route_ids.shape[1]
    flat_ids = route_ids.reshape(count_rows)
    onehot = (flat_ids[:, None] == jnp.arange(expert_count, dtype=jnp.int32)[None, :]).astype(
        jnp.int32
    )
    rank_table = jnp.cumsum(onehot, axis=0) - 1
    slot_in = jnp.sum(rank_table * onehot, axis=1)
    position = flat_ids * capacity + slot_in
    source = jnp.full((expert_count * capacity,), count_rows, jnp.int32)
    source = source.at[position].set(jnp.arange(count_rows, dtype=jnp.int32))
    return (position, source)


def gather_rows(values, source):
    padded = jnp.concatenate([values, jnp.zeros((1, values.shape[1]), values.dtype)], axis=0)
    return padded[source]


def forward_partial(row_block, gate_here, up_here, down_here):
    gate_pre = jnp.dot(row_block, gate_here, preferred_element_type=jnp.float32)
    up_pre = jnp.dot(row_block, up_here, preferred_element_type=jnp.float32)
    activated = (jax.nn.silu(gate_pre) * up_pre).astype(jnp.bfloat16)
    return jnp.dot(activated, down_here, preferred_element_type=jnp.float32).astype(jnp.bfloat16)


def backward_partial(row_block, grad_block, gate_here, up_here, down_here):
    gate_pre = jnp.dot(row_block, gate_here, preferred_element_type=jnp.float32)
    up_pre = jnp.dot(row_block, up_here, preferred_element_type=jnp.float32)
    sigmoid_gate = jax.nn.sigmoid(gate_pre)
    silu_value = jax.nn.silu(gate_pre)
    grad_act = jnp.einsum("md,hd->mh", grad_block, down_here, preferred_element_type=jnp.float32)
    grad_gate_pre = (
        grad_act * up_pre * sigmoid_gate * (1.0 + gate_pre * (1.0 - sigmoid_gate))
    ).astype(jnp.bfloat16)
    grad_up_pre = (grad_act * silu_value).astype(jnp.bfloat16)
    grad_rows = jnp.einsum(
        "mh,dh->md", grad_gate_pre, gate_here, preferred_element_type=jnp.float32
    )
    grad_rows = grad_rows + jnp.einsum(
        "mh,dh->md", grad_up_pre, up_here, preferred_element_type=jnp.float32
    )
    return grad_rows.astype(jnp.bfloat16)


def add_pair(first, second):
    return (first.astype(jnp.float32) + second.astype(jnp.float32)).astype(jnp.bfloat16)


def shards(
    fwd_state,
    new_tokens,
    saved_input,
    grad_state,
    new_grads,
    norm_gain,
    w_gate,
    w_up,
    w_down,
    fwd_ids,
    fwd_gates,
    bwd_ids,
    bwd_gates,
):
    gate_here = w_gate[0]
    up_here = w_up[0]
    down_here = w_down[0]
    gain_row = norm_gain[0]
    device_count = lax.axis_size("expert")
    expert_count = device_count // 2
    section_count = lax.axis_size("pipe")
    section_index = lax.axis_index("pipe")
    token_rows = fwd_state.shape[1]
    width = fwd_state.shape[2]
    topk_count = fwd_ids.shape[3]
    capacity = token_rows * topk_count // expert_count
    ticks_count = saved_input.shape[0]
    current = fwd_state[0]
    cotangent = grad_state[0]
    for step_index in range(ticks_count):
        normed, widened, unused_rms = normalize(current, gain_row)
        fwd_position, fwd_source = route_slots(fwd_ids[step_index, 0], capacity, expert_count)
        send_fwd = gather_rows(normed, fwd_source // topk_count).reshape(
            expert_count, capacity, width
        )
        saved_normed, saved_wide, inverse_rms = normalize(saved_input[step_index, 0], gain_row)
        bwd_position, bwd_source = route_slots(bwd_ids[step_index, 0], capacity, expert_count)
        send_rows = gather_rows(saved_normed, bwd_source // topk_count).reshape(
            expert_count, capacity, width
        )
        cot_wide = cotangent.astype(jnp.float32)
        row_grads = (
            jnp.repeat(cot_wide, topk_count, axis=0) * bwd_gates[step_index, 0].reshape(-1, 1)
        ).astype(jnp.bfloat16)
        send_grads = gather_rows(row_grads, bwd_source).reshape(expert_count, capacity, width)
        forward_copies = jnp.repeat(send_fwd, 2, axis=0)
        forward_arrived = lax.all_to_all(
            forward_copies, "expert", split_axis=0, concat_axis=0, tiled=True
        )
        forward_partial_value = forward_partial(
            forward_arrived.reshape(-1, width), gate_here, up_here, down_here
        ).reshape(device_count, capacity, width)
        forward_back = lax.all_to_all(
            forward_partial_value, "expert", split_axis=0, concat_axis=0, tiled=True
        )
        forward_paired = forward_back.reshape(expert_count, 2, capacity, width)
        back_fwd = add_pair(forward_paired[:, 0], forward_paired[:, 1]).reshape(
            expert_count * capacity, width
        )
        stacked = jnp.stack([send_rows, send_grads])
        copies = jnp.repeat(stacked, 2, axis=1)
        arrived = lax.all_to_all(copies, "expert", split_axis=1, concat_axis=1, tiled=True)
        partial_value = backward_partial(
            arrived[0].reshape(-1, width),
            arrived[1].reshape(-1, width),
            gate_here,
            up_here,
            down_here,
        )
        back = lax.all_to_all(
            partial_value.reshape(device_count, capacity, width),
            "expert",
            split_axis=0,
            concat_axis=0,
            tiled=True,
        )
        paired = back.reshape(expert_count, 2, capacity, width)
        back_bwd = add_pair(paired[:, 0], paired[:, 1]).reshape(expert_count * capacity, width)
        picked = back_fwd[fwd_position].astype(jnp.float32).reshape(token_rows, topk_count, width)
        mixture = jnp.sum(picked * fwd_gates[step_index, 0][:, :, None], axis=1)
        produced = (widened + mixture).astype(jnp.bfloat16)
        returned = back_bwd[bwd_position].astype(jnp.float32)
        grad_normed = jnp.sum(returned.reshape(token_rows, topk_count, width), axis=1)
        weighted = grad_normed * gain_row
        correction = jnp.mean(weighted * saved_wide, axis=-1, keepdims=True)
        grad_input = (
            cot_wide + inverse_rms * weighted - saved_wide * inverse_rms**3 * correction
        ).astype(jnp.bfloat16)
        if step_index + 1 < ticks_count:
            moved_rows = shifted(produced, "pipe", 1)
            current = jnp.where(section_index == 0, new_tokens[step_index], moved_rows)
            passed_back = shifted(grad_input, "pipe", -1)
            cotangent = jnp.where(
                section_index == section_count - 1, new_grads[step_index], passed_back
            )
    return (produced[None], grad_input[None])


def solution(mesh):
    placed = (
        P("pipe", "expert", None),
        P(None, "expert", None),
        P(None, "pipe", "expert", None),
        P("pipe", "expert", None),
        P(None, "expert", None),
        P("pipe", None),
        P("pipe", None, "expert"),
        P("pipe", None, "expert"),
        P("pipe", "expert", None),
        P(None, "pipe", "expert", None),
        P(None, "pipe", "expert", None),
        P(None, "pipe", "expert", None),
        P(None, "pipe", "expert", None),
    )
    return jax.shard_map(
        shards,
        mesh=mesh,
        in_specs=placed,
        out_specs=(P("pipe", "expert", None), P("pipe", "expert", None)),
        check_vma=False,
    )
```

profile of v0, /device:TPU:1, one launch (start us, length us, event | category | flops | bytes accessed | tf_op | source)
XLA Modules:
  0.0 604.0 jit_solution(10944091748381746438)
XLA Ops:
  17.1 95.0 %all_to_all.40 = bf16[2,32,8,3584]{3,2,0,1:T(8,128)(2,1)S(1)} all-to-all(bf16[2,32,8,3584]{3,2,0,1:T(8,128)(2,1)S(1)} %bitcast.266), channel_id=1, replica_groups=mesh['pipe'=8,'expert'=32] {'expert'}, dimensions={1} | all-to-all | bytes 7340032 | tf_op jit(solution)/shard_map/all_to_all | solution.py:131
  116.6 7.7 %fusion.26 = f32[256,3584]{1,0:T(8,128)} fusion(bf16[1,3584,512]{2,1,0:T(8,128)(2,1)} %param.19, f32[256,512]{1,0:T(8,128)S(1)} %fusion.8, bf16[1,3584,512]{2,1,0:T(8,128)(2,1)} %param.20, bf16[2,32,8,3584]{3,2,0,1:T(8,128)(2,1)} %copy-done.5, f32[256,512]{1,0:T(8,128)S(1)} %fusion.28), kind=kOutput, calls=%fused_computation.44 | convolution fusion | flops 1880358912 | bytes 13893632 | tf_op jit(solution)/shard_map/mh,dh->md/dot_general | solution.py:56
  124.3 5.6 fusion.5
  129.9 5.9 all-to-all-start.5
  138.4 41.3 %all-to-all-done.5 = bf16[32,8,3584]{2,1,0:T(8,128)(2,1)S(1)} async-done(((bf16[32,8,3584]{2,1,0:T(8,128)(2,1)}), bf16[32,8,3584]{2,1,0:T(8,128)(2,1)S(1)}, u32[]{:S(2)}, u32[]{:S(2)}) %all-to-all-start.5) | async-done | bytes 1835040 | tf_op jit(solution)/shard_map/all_to_all | solution.py:139
  180.0 2.1 gather_fusion.6
  188.0 6.7 %collective-permute-done.1 = bf16[32,3584]{1,0:T(8,128)(2,1)S(1)} collective-permute-done((bf16[32,3584]{1,0:T(8,128)(2,1)S(1)}, bf16[32,3584]{1,0:T(8,128)(2,1)S(1)}, u32[]{:S(2)}, u32[]{:S(2)}) %collective-permute-start.1) | collective-permute-done | bytes 229408 | tf_op jit(solution)/shard_map/ppermute | solution.py:10
  201.1 91.3 %all_to_all.41 = bf16[2,32,8,3584]{3,2,0,1:T(8,128)(2,1)S(1)} all-to-all(bf16[2,32,8,3584]{3,2,0,1:T(8,128)(2,1)S(1)} %bitcast.267), channel_id=1, replica_groups=mesh['pipe'=8,'expert'=32] {'expert'}, dimensions={1} | all-to-all | bytes 7340032 | tf_op jit(solution)/shard_map/all_to_all | solution.py:131
  296.9 7.7 %fusion.22 = f32[256,3584]{1,0:T(8,128)} fusion(bf16[1,3584,512]{2,1,0:T(8,128)(2,1)} %param.19, f32[256,512]{1,0:T(8,128)S(1)} %fusion.6, bf16[1,3584,512]{2,1,0:T(8,128)(2,1)} %param.20, bf16[2,32,8,3584]{3,2,0,1:T(8,128)(2,1)} %copy-done.6, f32[256,512]{1,0:T(8,128)S(1)} %fusion.24), kind=kOutput, calls=%fused_computation.40 | convolution fusion | flops 1880358912 | bytes 13893632 | tf_op jit(solution)/shard_map/mh,dh->md/dot_general | solution.py:56
  304.6 5.6 fusion.4
  310.2 6.4 %all-to-all-start.7 = ((bf16[32,8,3584]{2,1,0:T(8,128)(2,1)}), bf16[32,8,3584]{2,1,0:T(8,128)(2,1)S(1)}, u32[]{:S(2)}, u32[]{:S(2)}) async-start(bf16[32,8,3584]{2,1,0:T(8,128)(2,1)} %fusion.4), calls=%async_computation.7 | async-start | bytes 3670016 | tf_op jit(solution)/shard_map/all_to_all | solution.py:139
  318.7 41.7 %all-to-all-done.7 = bf16[32,8,3584]{2,1,0:T(8,128)(2,1)S(1)} async-done(((bf16[32,8,3584]{2,1,0:T(8,128)(2,1)}), bf16[32,8,3584]{2,1,0:T(8,128)(2,1)S(1)}, u32[]{:S(2)}, u32[]{:S(2)}) %all-to-all-start.7) | async-done | bytes 1835040 | tf_op jit(solution)/shard_map/all_to_all | solution.py:139
  360.6 2.1 gather_fusion.9
  367.1 49.2 %all_to_all.42 = bf16[32,8,3584]{2,1,0:T(8,128)(2,1)S(1)} all-to-all(bf16[32,8,3584]{2,1,0:T(8,128)(2,1)S(1)} %bitcast.272), channel_id=1, replica_groups=mesh['pipe'=8,'expert'=32] {'expert'}, dimensions={0} | all-to-all | bytes 3670016 | tf_op jit(solution)/shard_map/all_to_all | solution.py:116
  417.4 6.6 %fusion.2 = bf16[32,8,3584]{2,1,0:T(8,128)(2,1)} fusion(bf16[1,512,3584]{2,1,0:T(8,128)(2,1)} %param.21, bf16[1,3584,512]{2,1,0:T(8,128)(2,1)} %param.20, bf16[32,8,3584]{2,1,0:T(8,128)(2,1)S(1)} %all_to_all.42, f32[256,512]{1,0:T(8,128)S(1)} %fusion.32), kind=kOutput, calls=%fused_computation.20 | convolution fusion | flops 1880752128 | bytes 11534336 | tf_op jit(solution)/shard_map/dot_general | solution.py:43
  424.0 6.2 %all-to-all-start.1 = ((bf16[32,8,3584]{2,1,0:T(8,128)(2,1)}), bf16[32,8,3584]{2,1,0:T(8,128)(2,1)S(1)}, u32[]{:S(2)}, u32[]{:S(2)}) async-start(bf16[32,8,3584]{2,1,0:T(8,128)(2,1)} %fusion.2), calls=%async_computation.1 | async-start | bytes 3670016 | tf_op jit(solution)/shard_map/all_to_all | solution.py:122
  432.1 41.9 %all-to-all-done.1 = bf16[32,8,3584]{2,1,0:T(8,128)(2,1)S(1)} async-done(((bf16[32,8,3584]{2,1,0:T(8,128)(2,1)}), bf16[32,8,3584]{2,1,0:T(8,128)(2,1)S(1)}, u32[]{:S(2)}, u32[]{:S(2)}) %all-to-all-start.1) | async-done | bytes 1835040 | tf_op jit(solution)/shard_map/all_to_all | solution.py:122
  477.3 5.5 collective-permute-start
  482.8 3.3 collective-permute-done
  489.5 50.6 %all_to_all.43 = bf16[32,8,3584]{2,1,0:T(8,128)(2,1)S(1)} all-to-all(bf16[32,8,3584]{2,1,0:T(8,128)(2,1)S(1)} %bitcast.273), channel_id=1, replica_groups=mesh['pipe'=8,'expert'=32] {'expert'}, dimensions={0} | all-to-all | bytes 3670016 | tf_op jit(solution)/shard_map/all_to_all | solution.py:116
  541.2 6.6 %fusion.3 = bf16[32,8,3584]{2,1,0:T(8,128)(2,1)} fusion(bf16[1,512,3584]{2,1,0:T(8,128)(2,1)} %param.21, bf16[1,3584,512]{2,1,0:T(8,128)(2,1)} %param.20, bf16[32,8,3584]{2,1,0:T(8,128)(2,1)S(1)} %all_to_all.43, f32[256,512]{1,0:T(8,128)S(1)} %fusion.30), kind=kOutput, calls=%fused_computation.21 | convolution fusion | flops 1880752128 | bytes 11534336 | tf_op jit(solution)/shard_map/dot_general | solution.py:43
  547.8 6.0 all-to-all-start.3
  553.9 43.8 %all-to-all-done.3 = bf16[32,8,3584]{2,1,0:T(8,128)(2,1)S(1)} async-done(((bf16[32,8,3584]{2,1,0:T(8,128)(2,1)}), bf16[32,8,3584]{2,1,0:T(8,128)(2,1)S(1)}, u32[]{:S(2)}, u32[]{:S(2)}) %all-to-all-start.3) | async-done | bytes 1835040 | tf_op jit(solution)/shard_map/all_to_all | solution.py:122
  597.9 2.1 gather_fusion.3
  (189 shorter events, 61.5 us)
Async XLA Ops:
  6.0 6.1 %copy-start.18 = (f32[32]{0:T(128)}, f32[32]{0:T(128)S(1)}, u32[]{:S(2)}) copy-start(f32[32]{0:T(128)S(1)} %get-tuple-element.29) | copy-start | bytes 388
  10.0 2.1 copy-start
  17.1 95.0 %copy-start.25 = (bf16[1,3584,512]{2,1,0:T(8,128)(2,1)S(1)}, bf16[1,3584,512]{2,1,0:T(8,128)(2,1)}, u32[]{:S(2)}) copy-start(bf16[1,3584,512]{2,1,0:T(8,128)(2,1)} %param.19) | copy-start | bytes 11010052
  112.1 3.4 copy-start.29
  129.9 6.0 copy-start.15
  129.9 6.2 %copy-start.14 = (s32[1,1,32,4]{2,3,1,0:T(4,128)S(1)}, s32[1,1,32,4]{2,3,1,0:T(4,128)}, u32[]{:S(2)}) copy-start(s32[1,1,32,4]{2,3,1,0:T(4,128)} %get-tuple-element.12) | copy-start | bytes 1540
  129.9 6.6 %copy-start.13 = (s32[1,1,32,4]{2,3,1,0:T(4,128)S(1)}, s32[1,1,32,4]{2,3,1,0:T(4,128)}, u32[]{:S(2)}) copy-start(s32[1,1,32,4]{2,3,1,0:T(4,128)} %get-tuple-element.14) | copy-start | bytes 1540
  129.9 8.5 %copy-start.22 = (s32[128]{0:T(128)S(1)}, s32[128]{0:T(128)}, u32[]{:S(2)}) copy-start(s32[128]{0:T(128)} %copy-done.21) | copy-start | bytes 1540
  129.9 49.8 %all-to-all-start.5 = ((bf16[32,8,3584]{2,1,0:T(8,128)(2,1)}), bf16[32,8,3584]{2,1,0:T(8,128)(2,1)S(1)}, u32[]{:S(2)}, u32[]{:S(2)}) async-start(bf16[32,8,3584]{2,1,0:T(8,128)(2,1)} %fusion.5), calls=%async_computation.5 | async-start | bytes 3670016 | tf_op jit(solution)/shard_map/all_to_all | solution.py:139
  185.5 9.2 %collective-permute-start.1 = (bf16[32,3584]{1,0:T(8,128)(2,1)S(1)}, bf16[32,3584]{1,0:T(8,128)(2,1)S(1)}, u32[]{:S(2)}, u32[]{:S(2)}) collective-permute-start(bf16[32,3584]{1,0:T(8,128)(2,1)S(1)} %get-tuple-element.7), channel_id=1, source_target_pairs={{32,0},{64,32},{96,64},{128,96},{160,128},{192,160},{224,192},{33,... | collective-permute-start | bytes 688136 | tf_op jit(solution)/shard_map/ppermute | solution.py:10
  186.9 7.8 %copy-start.11 = (bf16[1,32,3584]{2,1,0:T(8,128)(2,1)S(1)}, bf16[1,32,3584]{2,1,0:T(8,128)(2,1)}, u32[]{:S(2)}) copy-start(bf16[1,32,3584]{2,1,0:T(8,128)(2,1)} %param.17) | copy-start | bytes 688132
  201.1 91.3 %copy-start.26 = (bf16[1,3584,512]{2,1,0:T(8,128)(2,1)S(1)}, bf16[1,3584,512]{2,1,0:T(8,128)(2,1)}, u32[]{:S(2)}) copy-start(bf16[1,3584,512]{2,1,0:T(8,128)(2,1)} %param.19) | copy-start | bytes 11010052
  292.4 3.4 copy-start.30
  310.2 6.4 %copy-start.16 = (s32[2,1,32,4]{2,3,1,0:T(4,128)S(1)}, s32[2,1,32,4]{2,3,1,0:T(4,128)}, u32[]{:S(2)}) copy-start(s32[2,1,32,4]{2,3,1,0:T(4,128)} %param.22) | copy-start | bytes 3076
  310.2 8.3 %copy-start.7 = (bf16[1,32,3584]{2,1,0:T(8,128)(2,1)S(1)}, bf16[1,32,3584]{2,1,0:T(8,128)(2,1)}, u32[]{:S(2)}) copy-start(bf16[1,32,3584]{2,1,0:T(8,128)(2,1)} %param.13) | copy-start | bytes 688132
  310.2 50.2 %all-to-all-start.7 = ((bf16[32,8,3584]{2,1,0:T(8,128)(2,1)}), bf16[32,8,3584]{2,1,0:T(8,128)(2,1)S(1)}, u32[]{:S(2)}, u32[]{:S(2)}) async-start(bf16[32,8,3584]{2,1,0:T(8,128)(2,1)} %fusion.4), calls=%async_computation.7 | async-start | bytes 3670016 | tf_op jit(solution)/shard_map/all_to_all | solution.py:139
  367.1 49.2 %copy-start.27 = (bf16[1,3584,512]{2,1,0:T(8,128)(2,1)S(1)}, bf16[1,3584,512]{2,1,0:T(8,128)(2,1)}, u32[]{:S(2)}) copy-start(bf16[1,3584,512]{2,1,0:T(8,128)(2,1)} %param.19) | copy-start | bytes 11010052
  424.0 6.2 %copy-start.17 = (f32[2,1,32,4]{2,3,1,0:T(4,128)S(1)}, f32[2,1,32,4]{2,3,1,0:T(4,128)}, u32[]{:S(2)}) copy-start(f32[2,1,32,4]{2,3,1,0:T(4,128)} %param.23) | copy-start | bytes 3076
  424.0 50.1 %all-to-all-start.1 = ((bf16[32,8,3584]{2,1,0:T(8,128)(2,1)}), bf16[32,8,3584]{2,1,0:T(8,128)(2,1)S(1)}, u32[]{:S(2)}, u32[]{:S(2)}) async-start(bf16[32,8,3584]{2,1,0:T(8,128)(2,1)} %fusion.2), calls=%async_computation.1 | async-start | bytes 3670016 | tf_op jit(solution)/shard_map/all_to_all | solution.py:122
  476.0 11.3 %copy-start.2 = (f32[32,3584]{1,0:T(8,128)S(1)}, f32[32,3584]{1,0:T(8,128)}, u32[]{:S(2)}) copy-start(f32[32,3584]{1,0:T(8,128)} %copy-done.1) | copy-start | bytes 1376260
  476.0 11.3 %copy-start.4 = (f32[32,3584]{1,0:T(8,128)S(1)}, f32[32,3584]{1,0:T(8,128)}, u32[]{:S(2)}) copy-start(f32[32,3584]{1,0:T(8,128)} %copy-done.3) | copy-start | bytes 1376260
  477.3 8.8 %collective-permute-start = (bf16[32,3584]{1,0:T(8,128)(2,1)S(1)}, bf16[32,3584]{1,0:T(8,128)(2,1)S(1)}, u32[]{:S(2)}, u32[]{:S(2)}) collective-permute-start(bf16[32,3584]{1,0:T(8,128)(2,1)S(1)} %fusion.121), channel_id=1, source_target_pairs={{0,32},{32,64},{64,96},{96,128},{128,160},{160,192},{192,224},{1,3... | collective-permute-start | bytes 688136 | tf_op jit(solution)/shard_map/ppermute | solution.py:10
  489.5 50.7 %copy-start.28 = (bf16[1,3584,512]{2,1,0:T(8,128)(2,1)S(1)}, bf16[1,3584,512]{2,1,0:T(8,128)(2,1)}, u32[]{:S(2)}) copy-start(bf16[1,3584,512]{2,1,0:T(8,128)(2,1)} %param.19) | copy-start | bytes 11010052
  547.8 49.9 %all-to-all-start.3 = ((bf16[32,8,3584]{2,1,0:T(8,128)(2,1)}), bf16[32,8,3584]{2,1,0:T(8,128)(2,1)S(1)}, u32[]{:S(2)}, u32[]{:S(2)}) async-start(bf16[32,8,3584]{2,1,0:T(8,128)(2,1)} %fusion.3), calls=%async_computation.3 | async-start | bytes 3670016 | tf_op jit(solution)/shard_map/all_to_all | solution.py:122
  (13 other events, 16.1 us)
where the time goes:
time: 615 us; the launch traced here: 604 us
  blocking collectives  286 us (47%)
  waiting for transfers between devices  179 us (29%)
  matrix products  46.4 us (8%)
  local copies, waits for them, and re-layouts  42.7 us (7%)
  starting transfers between devices  31.3 us (5%)
  other arithmetic  16.9 us (3%)
    all_to_all x2, blocking collectives, shards(): lax.all_to_all(copies, 'expert', split_axis=1, concat_axis=1, tiled=True)  186 us
    all_to_all x2, blocking collectives, shards(): lax.all_to_all(forward_copies, 'expert', split_axis=0, concat_axis=0, til...  99.9 us
    all_to_all x2, waiting for transfers between devices, shards(): lax.all_to_all(forward_partial_value, 'expert', split_axis=0, concat_axis...  85.7 us
    all_to_all x2, waiting for transfers between devices, shards(): lax.all_to_all(partial_value.reshape(device_count, capacity, width), 'exp...  83 us
    dot_general x2, matrix products, backward_partial(): jnp.einsum('mh,dh->md', grad_gate_pre, gate_here, preferred_element_type=...  15.5 us
    dot_general x2, matrix products, forward_partial(): jnp.dot(activated, down_here, preferred_element_type=jnp.float32)  13.1 us
  transfers between devices with their start and end apart: 6, of which 6 were waited for; matrix products, arithmetic and copies ran while one was open for 1% of the time, Pallas kernels for 0%

commit v1 on v0

v1 whole, which is shorter than its diff:
```python
import functools

import jax
import jax.numpy as jnp
from jax import lax
from jax.experimental import pallas as pl
from jax.experimental.pallas import tpu as pltpu
from jax.sharding import PartitionSpec as P

MESH = pl.DeviceIdType.MESH
F32 = jnp.float32
BF16 = jnp.bfloat16


def kernel(
    fwd_state,
    new_tokens,
    saved_input,
    grad_state,
    new_grads,
    norm_gain,
    w_gate,
    w_up,
    w_down,
    fwd_ids,
    fwd_gates,
    bwd_ids,
    bwd_gates,
    fwd_out,
    grad_out,
    gate_w,
    up_w,
    down_w,
    send,
    recv,
    partial,
    pair_in,
    back_send,
    back,
    rows_a,
    rows_b,
    gate_pre,
    up_pre,
    grad_act,
    hid_a,
    hid_b,
    stage,
    moved,
    tokens,
    grads,
    weight_sem,
    row_send,
    row_recv,
    swap_send,
    swap_recv,
    pair_send,
    pair_recv,
    back_ssem,
    back_rsem,
    pipe_send,
    pipe_recv,
):
    pipe = lax.axis_index("pipe")
    sections = lax.axis_size("pipe")
    me = lax.axis_index("expert")
    chips = lax.axis_size("expert") // 2
    chip = me // 2
    core = me % 2
    other = chip * 2 + 1 - core
    width = fwd_state.shape[-1]
    token_rows = fwd_state.shape[-2]
    topk = fwd_ids.shape[-1]
    slots = send.shape[2]
    count = chips * slots
    hidden = gate_w.shape[1]
    wide = 512
    after = lax.rem(pipe + 1, sections)
    before = lax.rem(pipe + sections - 1, sections)

    weight_copies = [
        pltpu.make_async_copy(source.at[0], target, weight_sem.at[i])
        for i, (source, target) in enumerate(
            ((w_gate, gate_w), (w_up, up_w), (w_down, down_w))
        )
    ]
    for copy in weight_copies:
        copy.start()

    barrier = pltpu.get_barrier_semaphore()

    @pl.loop(1, chips)
    def _(j):
        peer = lax.rem(chip + j, chips) * 2 + core
        pl.semaphore_signal(barrier, inc=1, device_id={"expert": peer}, device_id_type=MESH)

    pl.semaphore_signal(barrier, inc=1, device_id={"expert": other}, device_id_type=MESH)
    pl.semaphore_signal(barrier, inc=1, device_id={"pipe": after}, device_id_type=MESH)
    pl.semaphore_signal(barrier, inc=1, device_id={"pipe": before}, device_id_type=MESH)

    def columns(i):
        return pl.ds(pl.multiple_of(i * wide, wide), wide)

    def slot_matrix(ids, gates):
        named = lax.broadcasted_iota(jnp.int32, (token_rows, count), 1) // slots
        place = lax.broadcasted_iota(jnp.int32, (token_rows, count), 1) % slots
        chosen = jnp.zeros((token_rows, count), F32)
        weight = jnp.zeros((token_rows, count), F32)
        for k in range(topk):
            hit = ids[:, k : k + 1] == named
            chosen = jnp.where(hit, 1.0, chosen)
            weight = jnp.where(hit, gates[:, k : k + 1], weight)
        row = lax.broadcasted_iota(jnp.int32, (token_rows, token_rows), 0)
        col = lax.broadcasted_iota(jnp.int32, (token_rows, token_rows), 1)
        earlier = jnp.where(col < row, 1.0, 0.0).astype(BF16)
        rank = jnp.dot(earlier, chosen.astype(BF16), preferred_element_type=F32)
        taken = jnp.where(rank == place.astype(F32), chosen, 0.0)
        return taken, taken * weight

    def normalize(values):
        widened = values.astype(F32)
        inverse = lax.rsqrt(jnp.mean(widened * widened, axis=-1, keepdims=True) + 1e-06)
        normed = (widened * inverse * norm_gain[...]).astype(BF16)
        return normed, inverse

    def row_copy(unit, j):
        target = lax.rem(chip + j, chips)
        return pltpu.make_async_remote_copy(
            src_ref=send.at[unit, target],
            dst_ref=recv.at[unit, core, chip],
            send_sem=row_send.at[unit, j],
            recv_sem=row_recv.at[unit, j],
            device_id={"expert": target * 2 + core},
            device_id_type=MESH,
        )

    def row_arrival(unit, j):
        source = lax.rem(chip + chips - j, chips)
        return pltpu.make_async_remote_copy(
            src_ref=send.at[unit, source],
            dst_ref=recv.at[unit, core, source],
            send_sem=row_send.at[unit, j],
            recv_sem=row_recv.at[unit, j],
            device_id={"expert": source * 2 + core},
            device_id_type=MESH,
        )

    def dispatch(unit, source, taken, weighted=None):
        select = jnp.transpose(taken).astype(BF16)
        scale = None
        if weighted is not None:
            scale = jnp.sum(jnp.transpose(weighted), axis=1, keepdims=True)

        @pl.loop(0, width // wide)
        def _(i):
            cut = columns(i)
            rows = jnp.dot(select, source[:, cut], preferred_element_type=F32)
            if scale is not None:
                rows = rows * scale
            send[unit, :, :, cut] = rows.reshape(chips, slots, wide).astype(BF16)

        @pl.loop(1, chips)
        def _(j):
            row_copy(unit, j).start()

        recv[unit, core, chip] = send[unit, chip]

    def swap_copy(unit):
        return pltpu.make_async_remote_copy(
            src_ref=recv.at[unit, core],
            dst_ref=recv.at[unit, core],
            send_sem=swap_send.at[unit],
            recv_sem=swap_recv.at[unit],
            device_id={"expert": other},
            device_id_type=MESH,
        )

    def swap_arrival(unit):
        return pltpu.make_async_remote_copy(
            src_ref=recv.at[unit, 1 - core],
            dst_ref=recv.at[unit, 1 - core],
            send_sem=swap_send.at[unit],
            recv_sem=swap_recv.at[unit],
            device_id={"expert": other},
            device_id_type=MESH,
        )

    def collect(unit):
        @pl.loop(1, chips)
        def _(j):
            row_arrival(unit, j).wait_recv()

        swap_copy(unit).start()

    def gather(unit, target):
        swap_arrival(unit).wait_recv()
        swap_copy(unit).wait_send()

        @pl.loop(0, width // wide)
        def _(i):
            cut = columns(i)
            block = recv[unit, :, :, :, cut].astype(F32)
            target[:, cut] = block.reshape(2 * count, wide).astype(BF16)

    def project():
        @pl.loop(0, hidden // 256)
        def _(i):
            cut = pl.ds(pl.multiple_of(i * 256, 256), 256)
            gate_pre[:, cut] = jnp.dot(rows_a[...], gate_w[:, cut], preferred_element_type=F32)
            up_pre[:, cut] = jnp.dot(rows_a[...], up_w[:, cut], preferred_element_type=F32)

    def split_store(i, values):
        partial[:, :, :, columns(i)] = values.reshape(2, chips, slots, wide).astype(BF16)

    def pair_copy(unit):
        return pltpu.make_async_remote_copy(
            src_ref=partial.at[1 - core],
            dst_ref=pair_in.at[unit],
            send_sem=pair_send.at[unit],
            recv_sem=pair_recv.at[unit],
            device_id={"expert": other},
            device_id_type=MESH,
        )

    def back_copy(unit, j):
        target = lax.rem(chip + j, chips)
        return pltpu.make_async_remote_copy(
            src_ref=back_send.at[unit, target],
            dst_ref=back.at[unit, chip],
            send_sem=back_ssem.at[unit, j],
            recv_sem=back_rsem.at[unit, j],
            device_id={"expert": target * 2 + core},
            device_id_type=MESH,
        )

    def back_arrival(unit, j):
        source = lax.rem(chip + chips - j, chips)
        return pltpu.make_async_remote_copy(
            src_ref=back_send.at[unit, source],
            dst_ref=back.at[unit, source],
            send_sem=back_ssem.at[unit, j],
            recv_sem=back_rsem.at[unit, j],
            device_id={"expert": source * 2 + core},
            device_id_type=MESH,
        )

    def send_back(unit):
        copy = pair_copy(unit)
        copy.start()
        copy.wait()

        @pl.loop(0, width // wide)
        def _(i):
            cut = columns(i)
            both = partial[core, :, :, cut].astype(F32) + pair_in[unit, :, :, cut].astype(F32)
            back_send[unit, :, :, cut] = both.astype(BF16)

        @pl.loop(1, chips)
        def _(j):
            back_copy(unit, j).start()

        back[unit, chip] = back_send[unit, chip]

    def forward(unit):
        project()
        gate = gate_pre[...]
        hid_a[...] = (gate * jax.nn.sigmoid(gate) * up_pre[...]).astype(BF16)

        @pl.loop(0, width // wide)
        def _(i):
            split_store(
                i, jnp.dot(hid_a[...], down_w[:, columns(i)], preferred_element_type=F32)
            )

    def backward(unit):
        project()
        across = (((1,), (1,)), ((), ()))

        @pl.loop(0, hidden // 256)
        def _(i):
            cut = pl.ds(pl.multiple_of(i * 256, 256), 256)
            grad = lax.dot_general(rows_b[...], down_w[cut, :], across, preferred_element_type=F32)
            gate = gate_pre[:, cut]
            sigmoid = jax.nn.sigmoid(gate)
            hid_a[:, cut] = (
                grad * up_pre[:, cut] * sigmoid * (1.0 + gate * (1.0 - sigmoid))
            ).astype(BF16)
            hid_b[:, cut] = (grad * (gate * sigmoid)).astype(BF16)

        @pl.loop(0, width // wide)
        def _(i):
            total = lax.dot_general(
                hid_a[...], gate_w[columns(i), :], across, preferred_element_type=F32
            )
            total = total + lax.dot_general(
                hid_b[...], up_w[columns(i), :], across, preferred_element_type=F32
            )
            split_store(i, total)

    def returned(unit, matrices):
        @pl.loop(1, chips)
        def _(j):
            back_arrival(unit, j).wait_recv()

        @pl.loop(0, width // wide)
        def _(i):
            cut = columns(i)
            rows = back[unit, :, :, cut].astype(F32).reshape(count, wide).astype(BF16)
            total = jnp.zeros((token_rows, wide), F32)
            for matrix in matrices:
                total = total + jnp.dot(matrix, rows, preferred_element_type=F32)
            stage[:, cut] = total

    def mixture(unit, weighted, base, target):
        high = weighted.astype(BF16)
        low = (weighted - high.astype(F32)).astype(BF16)
        returned(unit, (high, low))
        target[...] = (base[...].astype(F32) + stage[...]).astype(BF16)

    def input_grad(unit, taken, saved, inverse, cotangent, target):
        returned(unit, (taken.astype(BF16),))
        weighted = stage[...] * norm_gain[...]
        widened = saved.astype(F32)
        correction = jnp.mean(weighted * widened, axis=-1, keepdims=True)
        target[...] = (
            cotangent[...].astype(F32)
            + inverse * weighted
            - widened * (inverse * inverse * inverse) * correction
        ).astype(BF16)

    def move(which, source, peer):
        return pltpu.make_async_remote_copy(
            src_ref=source,
            dst_ref=moved.at[which],
            send_sem=pipe_send.at[which],
            recv_sem=pipe_recv.at[which],
            device_id={"pipe": peer},
            device_id_type=MESH,
        )

    fwd_slots0 = slot_matrix(fwd_ids[0, 0], fwd_gates[0, 0])
    bwd_slots0 = slot_matrix(bwd_ids[0, 0], bwd_gates[0, 0])
    fwd_slots1 = slot_matrix(fwd_ids[1, 0], fwd_gates[1, 0])
    bwd_slots1 = slot_matrix(bwd_ids[1, 0], bwd_gates[1, 0])
    tokens[...] = normalize(fwd_state[0])[0]

    pl.semaphore_wait(barrier, chips + 2)
    dispatch(0, tokens, fwd_slots0[0])
    normed, inverse0 = normalize(saved_input[0, 0])
    tokens[...] = normed
    dispatch(1, tokens, bwd_slots0[0])
    dispatch(2, grad_state.at[0], *bwd_slots0)
    normed, inverse1 = normalize(saved_input[1, 0])
    tokens[...] = normed

    for copy in weight_copies:
        copy.wait()
    collect(0)
    gather(0, rows_a)
    forward(0)
    send_back(0)

    collect(1)
    collect(2)
    dispatch(3, tokens, bwd_slots1[0])
    gather(1, rows_a)
    gather(2, rows_b)
    backward(1)
    send_back(1)

    mixture(0, fwd_slots0[1], fwd_state.at[0], fwd_out.at[0])
    forth = move(0, fwd_out.at[0], after)
    forth.start()
    forth.wait()
    current = moved.at[0]
    current[...] = jnp.where(pipe == 0, new_tokens[0], current[...])
    tokens[...] = normalize(current[...])[0]
    dispatch(4, tokens, fwd_slots1[0])

    input_grad(1, bwd_slots0[0], saved_input[0, 0], inverse0, grad_state.at[0], grads)
    upward = move(1, grads, before)
    upward.start()
    upward.wait()
    cotangent = moved.at[1]
    cotangent[...] = jnp.where(pipe == sections - 1, new_grads[0], cotangent[...])
    dispatch(5, cotangent, *bwd_slots1)

    collect(3)
    collect(4)
    gather(4, rows_a)
    forward(2)
    send_back(2)

    collect(5)
    gather(3, rows_a)
    gather(5, rows_b)
    backward(3)
    send_back(3)

    mixture(2, fwd_slots1[1], current, fwd_out.at[0])
    input_grad(3, bwd_slots1[0], saved_input[1, 0], inverse1, cotangent, grad_out.at[0])

    for unit in range(6):

        @pl.loop(1, chips)
        def _(j):
            row_copy(unit, j).wait_send()

    for unit in range(4):

        @pl.loop(1, chips)
        def _(j):
            back_copy(unit, j).wait_send()


def shards(*arrays):
    fwd_state, fwd_ids, w_gate = arrays[0], arrays[9], arrays[6]
    token_rows, width = fwd_state.shape[1:]
    hidden = w_gate.shape[2]
    chips = lax.axis_size("expert") // 2
    slots = token_rows * fwd_ids.shape[3] // chips
    count = 2 * chips * slots
    dma = pltpu.SemaphoreType.DMA
    vmem = pl.BlockSpec(memory_space=pltpu.VMEM)
    hbm = pl.BlockSpec(memory_space=pl.ANY)
    row = jax.ShapeDtypeStruct(fwd_state.shape, BF16)
    return pl.pallas_call(
        kernel,
        out_shape=(row, row),
        in_specs=[vmem] * 6 + [hbm] * 3 + [vmem] * 4,
        out_specs=(vmem, vmem),
        scratch_shapes=[
            pltpu.VMEM((width, hidden), BF16),
            pltpu.VMEM((width, hidden), BF16),
            pltpu.VMEM((hidden, width), BF16),
            pltpu.VMEM((6, chips, slots, width), BF16),
            pltpu.VMEM((6, 2, chips, slots, width), BF16),
            pltpu.VMEM((2, chips, slots, width), BF16),
            pltpu.VMEM((4, chips, slots, width), BF16),
            pltpu.VMEM((4, chips, slots, width), BF16),
            pltpu.VMEM((4, chips, slots, width), BF16),
            pltpu.VMEM((count, width), BF16),
            pltpu.VMEM((count, width), BF16),
            pltpu.VMEM((count, hidden), F32),
            pltpu.VMEM((count, hidden), F32),
            pltpu.VMEM((8, 128), F32),
            pltpu.VMEM((count, hidden), BF16),
            pltpu.VMEM((count, hidden), BF16),
            pltpu.VMEM((token_rows, width), F32),
            pltpu.VMEM((2, token_rows, width), BF16),
            pltpu.VMEM((token_rows, width), BF16),
            pltpu.VMEM((token_rows, width), BF16),
            dma((3,)),
            dma((6, chips)),
            dma((6, chips)),
            dma((6,)),
            dma((6,)),
            dma((4,)),
            dma((4,)),
            dma((4, chips)),
            dma((4, chips)),
            dma((2,)),
            dma((2,)),
        ],
        compiler_params=pltpu.CompilerParams(
            collective_id=0, has_side_effects=True, vmem_limit_bytes=60 * 2**20
        ),
        name="relay",
    )(*arrays)


def solution(mesh):
    placed = (
        P("pipe", "expert", None),
        P(None, "expert", None),
        P(None, "pipe", "expert", None),
        P("pipe", "expert", None),
        P(None, "expert", None),
        P("pipe", None),
        P("pipe", None, "expert"),
        P("pipe", None, "expert"),
        P("pipe", "expert", None),
        P(None, "pipe", "expert", None),
        P(None, "pipe", "expert", None),
        P(None, "pipe", "expert", None),
        P(None, "pipe", "expert", None),
    )
    return jax.shard_map(
        shards,
        mesh=mesh,
        in_specs=placed,
        out_specs=(P("pipe", "expert", None), P("pipe", "expert", None)),
        check_vma=False,
    )
```

time: 615 us -> 229 us (0.37); the launches traced: 604 us -> 228 us
  blocking collectives: 286 us -> 0 us
  Pallas kernels: 0 us -> 219 us
  waiting for transfers between devices: 179 us -> 0 us
  matrix products: 46.4 us -> 0 us
  local copies, waits for them, and re-layouts: 42.7 us -> 8.82 us
  starting transfers between devices: 31.3 us -> 0 us
  other arithmetic: 16.9 us -> 0 us
    all_to_all x4 -> x0, blocking collectives: 286 us -> none  [the longest x2 186 us: shards(): lax.all_to_all(copies, 'expert', split_axis=1, concat_axis=1, tiled=True)]
    pallas_call x0 -> x1, Pallas kernels: none -> 219 us  [shards(): pl.pallas_call(kernel, out_shape=(row, row), in_specs=[vmem] * 6 + [hbm]...]
    all_to_all x4 -> x0, waiting for transfers between devices: 169 us -> none  [the longest x2 85.7 us: shards(): lax.all_to_all(forward_partial_value, 'expert', split_axis=0, concat_axis...]
    dot_general x12 -> x0, matrix products: 46.4 us -> none  [the longest x2 15.5 us: backward_partial(): jnp.einsum('mh,dh->md', grad_gate_pre, gate_here, preferred_element_type=...]
    all_to_all x4 -> x0, starting transfers between devices: 24.5 us -> none  [the longest x2 12.3 us: shards(): lax.all_to_all(partial_value.reshape(device_count, capacity, width), 'exp...]
    gather x10 -> x0, local copies, waits for them, and re-layouts: 14.1 us -> none  [the longest x6 6.81 us: gather_rows(): return padded[source]]
    ppermute x2 -> x0, waiting for transfers between devices: 9.95 us -> none  [shifted(): lax.ppermute(value, axis, [(source, source + steps) for source in range(f...]
    reduce_sum x13 -> x0, other arithmetic: 8.14 us -> none  [the longest x4 2.61 us: normalize(): jnp.mean(widened * widened, axis=-1, keepdims=True) + 1e-06]
  transfers between devices with their start and end apart: 6 -> 0, of which waited for: 6 -> 0; matrix products, arithmetic and copies ran while one was open for 1% -> 0% of each run, Pallas kernels for 0% -> 0%
where the time goes in v1:
time: 229 us; the launch traced here: 228 us
  Pallas kernels  219 us (96%)
  local copies, waits for them, and re-layouts  8.82 us (4%)
    pallas_call x1, Pallas kernels, shards(): pl.pallas_call(kernel, out_shape=(row, row), in_specs=[vmem] * 6 + [hbm]...  219 us
    unnamed x6, local copies, waits for them, and re-layouts  8.82 us

profile of v1, /device:TPU:1, one launch (start us, length us, event | category | flops | bytes accessed | tf_op | source)
XLA Modules:
  0.0 228.2 jit_solution(2592563037743311134)
XLA Ops:
  0.6 1.4 copy.15.fwd_ids
  2.0 1.4 copy.16.fwd_gates
  3.4 1.4 copy.17.bwd_ids
  4.8 1.4 copy.18.bwd_gates
  6.2 218.8 %relay.1 = (bf16[1,32,3584]{2,1,0:T(8,128)(2,1)}, bf16[1,32,3584]{2,1,0:T(8,128)(2,1)}) custom-call(bf16[1,32,3584]{2,1,0:T(8,128)(2,1)} %fwd_state.1, bf16[1,32,3584]{2,1,0:T(8,128)(2,1)} %new_tokens.1, bf16[2,1,32,3584]{3,2,1,0:T(8,128)(2,1)} %saved_input.1, bf16[1,32,3584]{2,1,0:T(8,128)(2,1)} %grad_state.1, bf16[1,32,3584]{2,1,0:T(8,128)(2,1)} %new_grads.1, ...), custom_call_target="tpu_custom_call" | custom-call | tf_op jit(solution)/shard_map/relay/pallas_call | solution.py:426
  224.9 1.6 copy.21
  226.6 1.6 copy.22

commit v2 on v1

v2 whole, which is shorter than its diff:
```python
import functools

import jax
import jax.numpy as jnp
from jax import lax
from jax.experimental import pallas as pl
from jax.experimental.pallas import tpu as pltpu
from jax.sharding import PartitionSpec as P

MESH = pl.DeviceIdType.MESH
F32 = jnp.float32
BF16 = jnp.bfloat16
PARTS = 2
BATCHES = (0, 1, 1, 3, 2, 3)
SCALED = (False, False, True, False, False, True)
LOTS = (0, 1, 2, 3, 0, 2)
FWD_UNITS, ROW_UNITS, GRAD_UNITS = (0, 4), (1, 3), (2, 5)
FAR_ROWS = (
    (0, 7, 0, 1),
    (1, 7, 1, 1),
    (0, 6, 0, 2),
    (0, 5, 0, -1),
    (1, 5, 1, -1),
    (1, 6, 1, -2),
)
FAR_STEPS = ((0, ((0, 1), (1, 1), (0, 2))), (4, ((0, -1), (1, -1), (1, -2))))

ORDER = (
    ("spread", 0),
    ("spread", 1),
    ("tables", 0),
    ("spread", 2),
    ("relay", 0, 0),
    ("relay", 0, 1),
    ("relay", 2, 0),
    ("relay", 1, 1),
    ("relay", 1, 0),
    ("finish", 0, 0),
    ("relay", 2, 1),
    ("finish", 0, 1),
    ("finish", 2, 0),
    ("spread", 3),
    ("finish", 1, 1),
    ("finish", 1, 0),
    ("collect", 0, 0),
    ("finish", 2, 1),
    ("collect", 0, 1),
    ("forward", 0),
    ("back", 0, 0),
    ("collect", 2, 0),
    ("relay", 3, 1),
    ("relay", 3, 0),
    ("collect", 1, 1),
    ("back", 0, 1),
    ("collect", 1, 0),
    ("recompute", 1),
    ("far", 0, 0),
    ("finish", 3, 1),
    ("collect", 2, 1),
    ("finish", 3, 0),
    ("backward", 1),
    ("far", 0, 1),
    ("back", 1, 1),
    ("collect", 3, 1),
    ("near", 0, 0),
    ("near", 0, 1),
    ("collect", 3, 0),
    ("back", 1, 0),
    ("recompute", 3),
    ("far", 1, 1),
    ("own", 0),
    ("far", 1, 0),
    ("near", 1, 1),
    ("near", 1, 0),
    ("spread", 4),
    ("own", 1),
    ("relay", 4, 0),
    ("relay", 4, 1),
    ("finish", 4, 0),
    ("spread", 5),
    ("finish", 4, 1),
    ("relay", 5, 0),
    ("relay", 5, 1),
    ("finish", 5, 0),
    ("collect", 4, 1),
    ("collect", 4, 0),
    ("finish", 5, 1),
    ("forward", 2),
    ("collect", 5, 1),
    ("collect", 5, 0),
    ("back", 2, 0),
    ("back", 2, 1),
    ("backward", 3),
    ("far", 2, 0),
    ("back", 3, 0),
    ("back", 3, 1),
    ("far", 2, 1),
    ("far", 3, 0),
    ("near", 2, 0),
    ("far", 3, 1),
    ("near", 2, 1),
    ("near", 3, 0),
    ("near", 3, 1),
    ("own", 2),
    ("own", 3),
)


def kernel(
    fwd_state,
    new_tokens,
    saved_input,
    grad_state,
    new_grads,
    norm_gain,
    w_gate,
    w_up,
    w_down,
    fwd_ids,
    fwd_gates,
    bwd_ids,
    bwd_gates,
    fwd_out,
    grad_out,
    gate_w,
    up_w,
    down_w,
    meta,
    table,
    held,
    cross,
    far,
    recv,
    partial,
    pair_in,
    results,
    cross_in,
    far_in,
    sums_in,
    sums_out,
    rows_in,
    fwd_gate,
    fwd_up,
    gate_pre,
    up_pre,
    hid_a,
    hid_b,
    stage,
    moved,
    grads,
    weight_sem,
    meta_send,
    meta_recv,
    row_send,
    row_recv,
    swap_send,
    swap_recv,
    pair_send,
    pair_recv,
    back_ssem,
    back_rsem,
    pipe_send,
    pipe_recv,
):
    pipe = lax.axis_index("pipe")
    sections = lax.axis_size("pipe")
    me = lax.axis_index("expert")
    chips = lax.axis_size("expert") // 2
    chip = me // 2
    core = me % 2
    ring = chips // 2
    column = chip // ring
    plane = chip % ring
    other = chip * 2 + 1 - core
    width = fwd_state.shape[-1]
    token_rows = fwd_state.shape[-2]
    topk = fwd_ids.shape[-1]
    slots = recv.shape[4]
    count = chips * slots
    hidden = gate_w.shape[1]
    wide = 256
    after = lax.rem(pipe + 1, sections)
    before = lax.rem(pipe + sections - 1, sections)

    weight_copies = [
        pltpu.make_async_copy(source.at[0], target, weight_sem.at[i])
        for i, (source, target) in enumerate(
            ((w_gate, gate_w), (w_up, up_w), (w_down, down_w))
        )
    ]
    for copy in weight_copies:
        copy.start()

    barrier = pltpu.get_barrier_semaphore()

    @pl.loop(1, chips)
    def _(j):
        peer = lax.rem(chip + j, chips) * 2 + core
        pl.semaphore_signal(barrier, inc=1, device_id={"expert": peer}, device_id_type=MESH)

    pl.semaphore_signal(barrier, inc=1, device_id={"expert": other}, device_id_type=MESH)
    pl.semaphore_signal(barrier, inc=1, device_id={"pipe": after}, device_id_type=MESH)
    pl.semaphore_signal(barrier, inc=1, device_id={"pipe": before}, device_id_type=MESH)

    def columns(i):
        return pl.ds(pl.multiple_of(i * wide, wide), wide)

    def part(half):
        return pl.ds(half * (width // PARTS), width // PARTS)

    def over_part(half):
        steps = width // PARTS // wide
        return pl.loop(half * steps, (half + 1) * steps, unroll=True)

    def device(across, step):
        to_column = lax.rem(column + across, 2)
        to_plane = lax.rem(plane + step + 2 * ring, ring)
        return (to_column * ring + to_plane) * 2 + core

    def expert(across, step):
        return device(across, step) // 2

    def remote(source, target, sends, receives, peer):
        return pltpu.make_async_remote_copy(
            src_ref=source,
            dst_ref=target,
            send_sem=sends,
            recv_sem=receives,
            device_id={"expert": peer},
            device_id_type=MESH,
        )

    def slot_weights(ids, gates):
        named = lax.broadcasted_iota(jnp.int32, (token_rows, count), 1) // slots
        place = lax.broadcasted_iota(jnp.int32, (token_rows, count), 1) % slots
        named = named.astype(F32)
        chosen = jnp.zeros((token_rows, count), F32)
        weight = jnp.zeros((token_rows, count), F32)
        for k in range(topk):
            hit = ids[:, k : k + 1] == named
            chosen = jnp.where(hit, 1.0, chosen)
            weight = jnp.where(hit, gates[:, k : k + 1], weight)
        row = lax.broadcasted_iota(jnp.int32, (token_rows, token_rows), 0)
        col = lax.broadcasted_iota(jnp.int32, (token_rows, token_rows), 1)
        earlier = jnp.where(col < row, 1.0, 0.0).astype(BF16)
        rank = jnp.dot(earlier, chosen.astype(BF16), preferred_element_type=F32)
        return jnp.where(rank == place.astype(F32), weight, 0.0)

    def inverse_rms(widened):
        return lax.rsqrt(jnp.mean(widened * widened, axis=-1, keepdims=True) + 1e-06)

    def normalize(values):
        widened = values.astype(F32)
        return (widened * inverse_rms(widened) * norm_gain[...]).astype(BF16)

    meta_copies = [
        remote(meta.at[2], meta.at[2 - step], meta_send.at[i], meta_recv.at[i], device(0, step))
        for i, step in enumerate((1, -1, 2, -2))
    ]

    def first_hop(unit, half):
        return [
            remote(
                held.at[unit, 2, :, part(half)],
                held.at[unit, 2 - step, :, part(half)],
                row_send.at[unit, half, i],
                row_recv.at[unit, half, i],
                device(0, step),
            )
            for i, step in enumerate((1, -1))
        ]

    def second_hop(unit, half):
        return [
            remote(
                held.at[unit, 2 - step, :, part(half)],
                held.at[unit, 2 - 2 * step, :, part(half)],
                row_send.at[unit, half, 2 + i],
                row_recv.at[unit, half, 2 + i],
                device(0, step),
            )
            for i, step in enumerate((1, -1))
        ]

    def cross_copies(unit, half):
        return [
            remote(
                cross.at[LOTS[unit], slots_of, :, part(half)],
                recv.at[unit, core, 1, slots_of, :, part(half)],
                row_send.at[unit, half, 4 + i],
                row_recv.at[unit, half, 4 + i],
                device(1, 0),
            )
            for i, slots_of in enumerate((pl.ds(1, 3), pl.ds(0, 1), pl.ds(4, 1)))
        ]

    def far_copies(unit, half):
        return [
            remote(
                far.at[LOTS[unit], i, :, part(half)],
                recv.at[unit, core, to, slot, :, part(half)],
                row_send.at[unit, half, 7 + i],
                row_recv.at[unit, half, 7 + i],
                device(across, step),
            )
            for i, (to, slot, across, step) in enumerate(FAR_ROWS)
        ]

    def pick(unit, half, first, many, targets):
        share = len(targets) // many
        batch, scaled = BATCHES[unit], SCALED[unit]
        picked = jnp.concatenate(
            [table[batch, first + n // share, e] for n, (e, _) in enumerate(targets)], axis=0
        )
        scale = jnp.sum(picked, axis=1, keepdims=True)
        if many > 1:
            picked = jnp.concatenate([picked] * many, axis=1)
            row = lax.broadcasted_iota(jnp.int32, picked.shape, 0) // (share * slots)
            col = lax.broadcasted_iota(jnp.int32, picked.shape, 1) // token_rows
            picked = jnp.where(row == col, picked, 0.0)
        select = jnp.where(picked > 0.0, 1.0, 0.0).astype(BF16)

        @over_part(half)
        def _(i):
            cut = columns(i)
            block = held[unit, pl.ds(first, many), :, cut].reshape(many * token_rows, wide)
            rows = jnp.dot(select, block, preferred_element_type=F32)
            if scaled:
                rows = rows * scale
            for n, (_, target) in enumerate(targets):
                target[:, cut] = rows[n * slots : (n + 1) * slots].astype(BF16)

    def near(unit, slot):
        return [
            (expert(0, 0), recv.at[unit, core, 0, slot]),
            (expert(1, 0), cross.at[LOTS[unit], slot]),
        ]

    def spread(unit):
        for half in range(PARTS):
            for copy in first_hop(unit, half):
                copy.start()

    def relay(unit, half):
        arrivals, onward = first_hop(unit, half), second_hop(unit, half)
        for i in range(2):
            arrivals[i].wait_recv()
            onward[i].start()
        targets = [target for slot in (1, 2, 3) for target in near(unit, slot)]
        pick(unit, half, 1, 3, targets)
        cross_copies(unit, half)[0].start()

    def finish(unit, half):
        arrivals, beyond = second_hop(unit, half), far_copies(unit, half)
        crossing = cross_copies(unit, half)
        for i, (slot, steps) in enumerate(FAR_STEPS):
            arrivals[i].wait_recv()
            targets = near(unit, slot) + [
                (expert(*at), far.at[LOTS[unit], 3 * i + n]) for n, at in enumerate(steps)
            ]
            pick(unit, half, slot, 1, targets)
            for n in range(3):
                beyond[3 * i + n].start()
            crossing[1 + i].start()

    def release(unit):
        for half in range(PARTS):
            for copy in cross_copies(unit, half) + far_copies(unit, half):
                copy.wait_send()

    def swap_copy(unit, half, rail):
        half_rows = recv.at[unit, rail, :, :, :, part(half)]
        return remote(
            half_rows, half_rows, swap_send.at[unit, half], swap_recv.at[unit, half], other
        )

    def collect(unit, half):
        for copy in cross_copies(unit, half) + far_copies(unit, half):
            copy.wait_recv()
        swap_copy(unit, half, core).start()

    def gather(unit):
        for half in range(PARTS):
            swap_copy(unit, half, 1 - core).wait_recv()
            swap_copy(unit, half, core).wait_send()

            @over_part(half)
            def _(i):
                cut = columns(i)
                block = recv[unit, :, :, :, :, cut].astype(F32)
                rows_in[:, cut] = block.reshape(2 * count, wide).astype(BF16)

    def project(gate_to, up_to):
        @pl.loop(0, hidden // 256)
        def _(i):
            cut = pl.ds(pl.multiple_of(i * 256, 256), 256)
            gate_to[:, cut] = jnp.dot(rows_in[...], gate_w[:, cut], preferred_element_type=F32)
            up_to[:, cut] = jnp.dot(rows_in[...], up_w[:, cut], preferred_element_type=F32)

    def pair_copy(unit, half):
        return remote(
            partial.at[unit % 2, 1 - core, :, :, :, part(half)],
            pair_in.at[unit, :, :, :, part(half)],
            pair_send.at[unit, half],
            pair_recv.at[unit, half],
            other,
        )

    def result_copies(unit, half):
        crossing = remote(
            results.at[unit, 1, pl.ds(0, 5), :, part(half)],
            cross_in.at[unit, :, :, part(half)],
            back_ssem.at[unit, half, 0],
            back_rsem.at[unit, half, 0],
            device(1, 0),
        )
        return [crossing] + [
            remote(
                results.at[unit, to, slot, :, part(half)],
                far_in.at[unit, i, :, part(half)],
                back_ssem.at[unit, half, 1 + i],
                back_rsem.at[unit, half, 1 + i],
                device(across, -step),
            )
            for i, (to, slot, across, step) in enumerate(FAR_ROWS)
        ]

    def sum_copies(unit, half, hop):
        return [
            remote(
                sums_out.at[unit % 2, hop, i, :, part(half)],
                sums_in.at[unit, hop, i, :, part(half)],
                back_ssem.at[unit, half, 7 + 2 * hop + i],
                back_rsem.at[unit, half, 7 + 2 * hop + i],
                device(0, step),
            )
            for i, step in enumerate((-1, 1))
        ]

    def combine(unit, half, slot, terms, added, put):
        gated = unit % 2 == 0
        weights = jnp.transpose(
            jnp.concatenate([table[unit, slot, e] for e, _ in terms], axis=0)
        )
        if gated:
            high = weights.astype(BF16)
            low = (weights - high.astype(F32)).astype(BF16)
            matrix = jnp.concatenate([high, low], axis=0)
        else:
            matrix = jnp.where(weights > 0.0, 1.0, 0.0).astype(BF16)

        @over_part(half)
        def _(i):
            cut = columns(i)
            rows = jnp.concatenate([term[:, cut].astype(F32) for _, term in terms], axis=0)
            total = jnp.dot(matrix, rows.astype(BF16), preferred_element_type=F32)
            if gated:
                total = total[:token_rows] + total[token_rows:]
            for extra in added:
                total = total + extra[:, cut].astype(F32)
            put(cut, total)

    def close_terms(unit, slot):
        return [
            (expert(0, 0), results.at[unit, 0, slot]),
            (expert(1, 0), cross_in.at[unit, slot]),
        ]

    def sum_far(unit, half):
        onward = sum_copies(unit, half, 0)
        for copy in result_copies(unit, half):
            copy.wait_recv()
        for i, (slot, steps) in enumerate(FAR_STEPS):
            terms = close_terms(unit, slot) + [
                (expert(*at), far_in.at[unit, 3 * i + n]) for n, at in enumerate(steps)
            ]
            target = sums_out.at[unit % 2, 0, i]

            def put(cut, total):
                target[:, cut] = total.astype(BF16)

            combine(unit, half, slot, terms, [], put)
            onward[i].start()

    def sum_near(unit, half):
        arrivals, onward = sum_copies(unit, half, 0), sum_copies(unit, half, 1)
        for i, slot in enumerate((1, 3)):
            arrivals[i].wait_recv()
            target = sums_out.at[unit % 2, 1, i]

            def put(cut, total):
                target[:, cut] = total.astype(BF16)

            terms = close_terms(unit, slot)
            combine(unit, half, slot, terms, [sums_in.at[unit, 0, i]], put)
            onward[i].start()

    def sum_own(unit):
        def put(cut, total):
            stage[:, cut] = total

        added = [sums_in.at[unit, 1, i] for i in range(2)]
        for half in range(PARTS):
            for copy in sum_copies(unit, half, 1):
                copy.wait_recv()
            combine(unit, half, 2, close_terms(unit, 2), added, put)

    def sums_sent(unit):
        for half in range(PARTS):
            for hop in range(2):
                for copy in sum_copies(unit, half, hop):
                    copy.wait_send()

    def send_back(unit, half):
        pair_copy(unit, half).wait()

        @over_part(half)
        def _(i):
            cut = columns(i)
            mine = partial[unit % 2, core, :, :, :, cut].astype(F32)
            both = mine + pair_in[unit, :, :, :, cut].astype(F32)
            results[unit, :, :, :, cut] = both.astype(BF16)

        for copy in result_copies(unit, half):
            copy.start()

    def outputs(unit, rows):
        for half in range(PARTS):

            @over_part(half)
            def _(i):
                values = rows(columns(i)).reshape(2, 2, ring, slots, wide)
                partial[unit % 2, :, :, :, :, columns(i)] = values.astype(BF16)

            pair_copy(unit, half).start()

    def forward(unit):
        gather(FWD_UNITS[unit // 2])
        project(fwd_gate, fwd_up)
        gate = fwd_gate[...]
        hid_a[...] = (gate * jax.nn.sigmoid(gate) * fwd_up[...]).astype(BF16)
        outputs(
            unit, lambda cut: jnp.dot(hid_a[...], down_w[:, cut], preferred_element_type=F32)
        )

    def recompute(unit):
        gather(ROW_UNITS[unit // 2])
        project(gate_pre, up_pre)

    def backward(unit):
        gather(GRAD_UNITS[unit // 2])
        across = (((1,), (1,)), ((), ()))

        @pl.loop(0, hidden // 256)
        def _(i):
            cut = pl.ds(pl.multiple_of(i * 256, 256), 256)
            grad = lax.dot_general(rows_in[...], down_w[cut, :], across, preferred_element_type=F32)
            gate = gate_pre[:, cut]
            sigmoid = jax.nn.sigmoid(gate)
            hid_a[:, cut] = (
                grad * up_pre[:, cut] * sigmoid * (1.0 + gate * (1.0 - sigmoid))
            ).astype(BF16)
            hid_b[:, cut] = (grad * (gate * sigmoid)).astype(BF16)

        def rows(cut):
            total = lax.dot_general(
                hid_a[...], gate_w[cut, :], across, preferred_element_type=F32
            )
            return total + lax.dot_general(
                hid_b[...], up_w[cut, :], across, preferred_element_type=F32
            )

        outputs(unit, rows)

    def mixture(unit, base, target):
        sum_own(unit)
        target[...] = (base[...].astype(F32) + stage[...]).astype(BF16)

    def input_grad(unit, saved, cotangent, target):
        sum_own(unit)
        weighted = stage[...] * norm_gain[...]
        widened = saved.astype(F32)
        inverse = inverse_rms(widened)
        correction = jnp.mean(weighted * widened, axis=-1, keepdims=True)
        target[...] = (
            cotangent[...].astype(F32)
            + inverse * weighted
            - widened * (inverse * inverse * inverse) * correction
        ).astype(BF16)

    def move(which, source, peer):
        return pltpu.make_async_remote_copy(
            src_ref=source,
            dst_ref=moved.at[which],
            send_sem=pipe_send.at[which],
            recv_sem=pipe_recv.at[which],
            device_id={"pipe": peer},
            device_id_type=MESH,
        )

    for batch, (ids, gates) in enumerate(
        ((fwd_ids, fwd_gates), (bwd_ids, bwd_gates), (fwd_ids, fwd_gates), (bwd_ids, bwd_gates))
    ):
        begin = 2 * topk * batch
        meta[2, :, begin : begin + topk] = ids[batch // 2, 0].astype(F32)
        meta[2, :, begin + topk : begin + 2 * topk] = gates[batch // 2, 0]
    current, cotangent = moved.at[0], moved.at[1]
    forth = move(0, fwd_out.at[0], after)
    upward = move(1, grads, before)

    def begin_spread(unit):
        if unit == 0:
            held[0, 2] = normalize(fwd_state[0])
            pl.semaphore_wait(barrier, chips + 2)
            for copy in meta_copies:
                copy.start()
        elif unit == 1:
            held[1, 2] = normalize(saved_input[0, 0])
        elif unit == 2:
            held[2, 2] = grad_state[0]
        elif unit == 3:
            held[3, 2] = normalize(saved_input[1, 0])
        elif unit == 4:
            forth.wait()
            current[...] = jnp.where(pipe == 0, new_tokens[0], current[...])
            held[4, 2] = normalize(current[...])
            release(0)
            sums_sent(0)
        else:
            upward.wait()
            cotangent[...] = jnp.where(pipe == sections - 1, new_grads[0], cotangent[...])
            held[5, 2] = cotangent[...]
            release(2)
            sums_sent(1)
        spread(unit)

    def tables(_):
        for copy in meta_copies:
            copy.wait_recv()

        @pl.loop(0, 5)
        def _(slot):
            for batch in range(4):
                begin = 2 * topk * batch
                weights = slot_weights(
                    meta[slot, :, begin : begin + topk],
                    meta[slot, :, begin + topk : begin + 2 * topk],
                )
                table[batch, slot] = jnp.transpose(weights).reshape(chips, slots, token_rows)

        for copy in weight_copies:
            copy.wait()

    def complete(unit):
        if unit == 0:
            mixture(0, fwd_state.at[0], fwd_out.at[0])
            forth.start()
        elif unit == 1:
            input_grad(1, saved_input[0, 0], grad_state.at[0], grads)
            upward.start()
        elif unit == 2:
            mixture(2, current, fwd_out.at[0])
        else:
            input_grad(3, saved_input[1, 0], cotangent, grad_out.at[0])

    steps = {
        "spread": begin_spread,
        "tables": tables,
        "relay": relay,
        "finish": finish,
        "collect": collect,
        "forward": forward,
        "recompute": recompute,
        "backward": backward,
        "back": send_back,
        "far": sum_far,
        "near": sum_near,
        "own": complete,
    }
    for name, *which in ORDER:
        steps[name](*which)

    for copy in meta_copies:
        copy.wait_send()
    for unit in range(6):
        for half in range(PARTS):
            for copy in first_hop(unit, half) + second_hop(unit, half):
                copy.wait_send()
    for unit in (4, 1, 5, 3):
        release(unit)
    for unit in (2, 3):
        sums_sent(unit)
    for unit in range(4):
        for half in range(PARTS):
            for copy in result_copies(unit, half):
                copy.wait_send()


def shards(*arrays):
    fwd_state, fwd_ids, w_gate = arrays[0], arrays[9], arrays[6]
    token_rows, width = fwd_state.shape[1:]
    hidden = w_gate.shape[2]
    chips = lax.axis_size("expert") // 2
    slots = token_rows * fwd_ids.shape[3] // chips
    count = 2 * chips * slots
    dma = pltpu.SemaphoreType.DMA
    vmem = pl.BlockSpec(memory_space=pltpu.VMEM)
    hbm = pl.BlockSpec(memory_space=pl.ANY)
    row = jax.ShapeDtypeStruct(fwd_state.shape, BF16)
    return pl.pallas_call(
        kernel,
        out_shape=(row, row),
        in_specs=[vmem] * 6 + [hbm] * 3 + [vmem] * 4,
        out_specs=(vmem, vmem),
        scratch_shapes=[
            pltpu.VMEM((width, hidden), BF16),
            pltpu.VMEM((width, hidden), BF16),
            pltpu.VMEM((hidden, width), BF16),
            pltpu.VMEM((5, token_rows, 128), F32),
            pltpu.VMEM((4, 5, chips, slots, token_rows), F32),
            pltpu.VMEM((6, 5, token_rows, width), BF16),
            pltpu.VMEM((4, 5, slots, width), BF16),
            pltpu.VMEM((4, 6, slots, width), BF16),
            pltpu.VMEM((6, 2, 2, chips // 2, slots, width), BF16),
            pltpu.VMEM((2, 2, 2, chips // 2, slots, width), BF16),
            pltpu.VMEM((4, 2, chips // 2, slots, width), BF16),
            pltpu.VMEM((4, 2, chips // 2, slots, width), BF16),
            pltpu.VMEM((4, 5, slots, width), BF16),
            pltpu.VMEM((4, 6, slots, width), BF16),
            pltpu.VMEM((4, 2, 2, token_rows, width), BF16),
            pltpu.VMEM((2, 2, 2, token_rows, width), BF16),
            pltpu.VMEM((count, width), BF16),
            pltpu.VMEM((count, hidden), F32),
            pltpu.VMEM((count, hidden), F32),
            pltpu.VMEM((count, hidden), F32),
            pltpu.VMEM((count, hidden), F32),
            pltpu.VMEM((count, hidden), BF16),
            pltpu.VMEM((count, hidden), BF16),
            pltpu.VMEM((token_rows, width), F32),
            pltpu.VMEM((2, token_rows, width), BF16),
            pltpu.VMEM((token_rows, width), BF16),
            dma((3,)),
            dma((4,)),
            dma((4,)),
            dma((6, PARTS, 13)),
            dma((6, PARTS, 13)),
            dma((6, PARTS)),
            dma((6, PARTS)),
            dma((4, PARTS)),
            dma((4, PARTS)),
            dma((4, PARTS, 11)),
            dma((4, PARTS, 11)),
            dma((2,)),
            dma((2,)),
        ],
        compiler_params=pltpu.CompilerParams(
            collective_id=0, has_side_effects=True, vmem_limit_bytes=60 * 2**20
        ),
        name="relay",
    )(*arrays)


def solution(mesh):
    placed = (
        P("pipe", "expert", None),
        P(None, "expert", None),
        P(None, "pipe", "expert", None),
        P("pipe", "expert", None),
        P(None, "expert", None),
        P("pipe", None),
        P("pipe", None, "expert"),
        P("pipe", None, "expert"),
        P("pipe", "expert", None),
        P(None, "pipe", "expert", None),
        P(None, "pipe", "expert", None),
        P(None, "pipe", "expert", None),
        P(None, "pipe", "expert", None),
    )
    return jax.shard_map(
        shards,
        mesh=mesh,
        in_specs=placed,
        out_specs=(P("pipe", "expert", None), P("pipe", "expert", None)),
        check_vma=False,
    )
```

time: 229 us -> 187 us (0.82)
  Pallas kernels: 219 us -> 178 us
    pallas_call x1, Pallas kernels: 219 us -> 178 us  [shards(): pl.pallas_call(kernel, out_shape=(row, row), in_specs=[vmem] * 6 + [hbm]...]
where the time goes in v2:
time: 187 us
  Pallas kernels  178 us (95%)
  local copies, waits for them, and re-layouts  8.82 us (5%)
    pallas_call x1, Pallas kernels, shards(): pl.pallas_call(kernel, out_shape=(row, row), in_specs=[vmem] * 6 + [hbm]...  178 us
    unnamed x6, local copies, waits for them, and re-layouts  8.82 us

profile of v2, /device:TPU:1, one launch (start us, length us, event | category | flops | bytes accessed | tf_op | source)
XLA Modules:
  0.0 187.2 jit_solution(3380904462789410048)
XLA Ops:
  0.6 1.4 copy.15.fwd_ids
  2.0 1.4 copy.16.fwd_gates
  3.4 1.4 copy.17.bwd_ids
  4.8 1.4 copy.18.bwd_gates
  6.2 177.7 %relay.1 = (bf16[1,32,3584]{2,1,0:T(8,128)(2,1)}, bf16[1,32,3584]{2,1,0:T(8,128)(2,1)}) custom-call(bf16[1,32,3584]{2,1,0:T(8,128)(2,1)} %fwd_state.1, bf16[1,32,3584]{2,1,0:T(8,128)(2,1)} %new_tokens.1, bf16[2,1,32,3584]{3,2,1,0:T(8,128)(2,1)} %saved_input.1, bf16[1,32,3584]{2,1,0:T(8,128)(2,1)} %grad_state.1, bf16[1,32,3584]{2,1,0:T(8,128)(2,1)} %new_grads.1, ...), custom_call_target="tpu_custom_call" | custom-call | tf_op jit(solution)/shard_map/relay/pallas_call | solution.py:710
  183.9 1.6 copy.21
  185.5 1.6 copy.22

commit v3 on v2

--- a/solution.py
+++ b/solution.py
@@ -26,83 +26,83 @@
 FAR_STEPS = ((0, ((0, 1), (1, 1), (0, 2))), (4, ((0, -1), (1, -1), (1, -2))))
 
 ORDER = (
+    ("spread", 2),
+    ("spread", 1),
     ("spread", 0),
-    ("spread", 1),
     ("tables", 0),
-    ("spread", 2),
+    ("relay", 2, 0),
+    ("relay", 2, 1),
+    ("relay", 1, 0),
+    ("relay", 1, 1),
+    ("finish", 2, 0),
+    ("finish", 1, 0),
+    ("finish", 1, 1),
+    ("finish", 2, 1),
     ("relay", 0, 0),
     ("relay", 0, 1),
-    ("relay", 2, 0),
-    ("relay", 1, 1),
-    ("relay", 1, 0),
+    ("spread", 3),
+    ("collect", 2, 0),
+    ("collect", 1, 0),
+    ("collect", 1, 1),
+    ("recompute", 1),
+    ("collect", 2, 1),
     ("finish", 0, 0),
-    ("relay", 2, 1),
     ("finish", 0, 1),
-    ("finish", 2, 0),
-    ("spread", 3),
-    ("finish", 1, 1),
-    ("finish", 1, 0),
+    ("backward", 1),
+    ("relay", 3, 0),
+    ("back", 1, 0),
+    ("back", 1, 1),
     ("collect", 0, 0),
-    ("finish", 2, 1),
     ("collect", 0, 1),
+    ("finish", 3, 0),
     ("forward", 0),
+    ("far", 1, 0),
+    ("back", 0, 1),
+    ("far", 1, 1),
     ("back", 0, 0),
-    ("collect", 2, 0),
+    ("collect", 3, 0),
+    ("near", 1, 0),
+    ("near", 1, 1),
+    ("far", 0, 1),
+    ("far", 0, 0),
+    ("own", 1),
     ("relay", 3, 1),
-    ("relay", 3, 0),
-    ("collect", 1, 1),
-    ("back", 0, 1),
-    ("collect", 1, 0),
-    ("recompute", 1),
-    ("far", 0, 0),
+    ("near", 0, 1),
+    ("near", 0, 0),
+    ("spread", 5),
     ("finish", 3, 1),
-    ("collect", 2, 1),
-    ("finish", 3, 0),
-    ("backward", 1),
-    ("far", 0, 1),
-    ("back", 1, 1),
-    ("collect", 3, 1),
-    ("near", 0, 0),
-    ("near", 0, 1),
-    ("collect", 3, 0),
-    ("back", 1, 0),
-    ("recompute", 3),
-    ("far", 1, 1),
     ("own", 0),
-    ("far", 1, 0),
-    ("near", 1, 1),
-    ("near", 1, 0),
-    ("spread", 4),
-    ("own", 1),
-    ("relay", 4, 0),
-    ("relay", 4, 1),
-    ("finish", 4, 0),
-    ("spread", 5),
-    ("finish", 4, 1),
     ("relay", 5, 0),
     ("relay", 5, 1),
+    ("spread", 4),
     ("finish", 5, 0),
+    ("relay", 4, 0),
+    ("finish", 5, 1),
+    ("collect", 3, 1),
+    ("recompute", 3),
+    ("relay", 4, 1),
+    ("collect", 5, 0),
+    ("finish", 4, 0),
+    ("collect", 5, 1),
+    ("finish", 4, 1),
+    ("backward", 3),
+    ("back", 3, 0),
     ("collect", 4, 1),
     ("collect", 4, 0),
-    ("finish", 5, 1),
+    ("back", 3, 1),
     ("forward", 2),
-    ("collect", 5, 1),
-    ("collect", 5, 0),
+    ("far", 3, 0),
     ("back", 2, 0),
     ("back", 2, 1),
-    ("backward", 3),
+    ("near", 3, 0),
+    ("far", 3, 1),
     ("far", 2, 0),
-    ("back", 3, 0),
-    ("back", 3, 1),
     ("far", 2, 1),
-    ("far", 3, 0),
+    ("near", 3, 1),
     ("near", 2, 0),
-    ("far", 3, 1),
     ("near", 2, 1),
-    ("near", 3, 0),
-    ("near", 3, 1),
+    ("own", 3),
     ("own", 2),
-    ("own", 3),
 )
 
 
@@ -122,6 +122,13 @@
     bwd_gates,
     fwd_out,
     grad_out,
+    inputs,
+    gain,
+    ids,
+    gates,
+    outs,
+    input_sem,
+    output_sem,
     gate_w,
     up_w,
     down_w,
@@ -148,7 +155,6 @@
     stage,
     moved,
     grads,
-    weight_sem,
     meta_send,
     meta_recv,
     row_send,
@@ -174,7 +180,7 @@
     other = chip * 2 + 1 - core
     width = fwd_state.shape[-1]
     token_rows = fwd_state.shape[-2]
-    topk = fwd_ids.shape[-1]
+    topk = fwd_ids.shape[-2]
     slots = recv.shape[4]
     count = chips * slots
     hidden = gate_w.shape[1]
@@ -182,15 +188,6 @@
     after = lax.rem(pipe + 1, sections)
     before = lax.rem(pipe + sections - 1, sections)
 
-    weight_copies = [
-        pltpu.make_async_copy(source.at[0], target, weight_sem.at[i])
-        for i, (source, target) in enumerate(
-            ((w_gate, gate_w), (w_up, up_w), (w_down, down_w))
-        )
-    ]
-    for copy in weight_copies:
-        copy.start()
-
     barrier = pltpu.get_barrier_semaphore()
 
     @pl.loop(1, chips)
@@ -201,6 +198,34 @@
     pl.semaphore_signal(barrier, inc=1, device_id={"expert": other}, device_id_type=MESH)
     pl.semaphore_signal(barrier, inc=1, device_id={"pipe": after}, device_id_type=MESH)
     pl.semaphore_signal(barrier, inc=1, device_id={"pipe": before}, device_id_type=MESH)
+
+    sources = {
+        "fwd_ids": (fwd_ids.at[:, 0], ids.at[0]),
+        "fwd_gates": (fwd_gates.at[:, 0], gates.at[0]),
+        "bwd_ids": (bwd_ids.at[:, 0], ids.at[1]),
+        "bwd_gates": (bwd_gates.at[:, 0], gates.at[1]),
+        "grad_state": (grad_state.at[0], held.at[2, 2]),
+        "gain": (norm_gain, gain),
+        "saved0": (saved_input.at[0, 0], inputs.at[2]),
+        "fwd_state": (fwd_state.at[0], inputs.at[0]),
+        "saved1": (saved_input.at[1, 0], inputs.at[3]),
+        "gate": (w_gate.at[0], gate_w),
+        "up": (w_up.at[0], up_w),
+        "down": (w_down.at[0], down_w),
+        "new_tokens": (new_tokens.at[0], inputs.at[1]),
+        "new_grads": (new_grads.at[0], inputs.at[4]),
+    }
+    loads = {
+        key: pltpu.make_async_copy(source, target, input_sem.at[i])
+        for i, (key, (source, target)) in enumerate(sources.items())
+    }
+    for load in loads.values():
+        load.start()
+
+    def need(*keys):
+        for key in keys:
+            if key in loads:
+                loads.pop(key).wait()
 
     def columns(i):
         return pl.ds(pl.multiple_of(i * wide, wide), wide)
@@ -231,19 +256,19 @@
         )
 
     def slot_weights(ids, gates):
-        named = lax.broadcasted_iota(jnp.int32, (token_rows, count), 1) // slots
-        place = lax.broadcasted_iota(jnp.int32, (token_rows, count), 1) % slots
+        named = lax.broadcasted_iota(jnp.int32, (count, token_rows), 0) // slots
+        place = lax.broadcasted_iota(jnp.int32, (count, token_rows), 0) % slots
         named = named.astype(F32)
-        chosen = jnp.zeros((token_rows, count), F32)
-        weight = jnp.zeros((token_rows, count), F32)
+        chosen = jnp.zeros((count, token_rows), F32)
+        weight = jnp.zeros((count, token_rows), F32)
         for k in range(topk):
-            hit = ids[:, k : k + 1] == named
+            hit = ids[k : k + 1] == named
             chosen = jnp.where(hit, 1.0, chosen)
-            weight = jnp.where(hit, gates[:, k : k + 1], weight)
+            weight = jnp.where(hit, gates[k : k + 1], weight)
         row = lax.broadcasted_iota(jnp.int32, (token_rows, token_rows), 0)
         col = lax.broadcasted_iota(jnp.int32, (token_rows, token_rows), 1)
-        earlier = jnp.where(col < row, 1.0, 0.0).astype(BF16)
-        rank = jnp.dot(earlier, chosen.astype(BF16), preferred_element_type=F32)
+        earlier = jnp.where(row < col, 1.0, 0.0).astype(BF16)
+        rank = jnp.dot(chosen.astype(BF16), earlier, preferred_element_type=F32)
         return jnp.where(rank == place.astype(F32), weight, 0.0)
 
     def inverse_rms(widened):
@@ -251,7 +276,7 @@
 
     def normalize(values):
         widened = values.astype(F32)
-        return (widened * inverse_rms(widened) * norm_gain[...]).astype(BF16)
+        return (widened * inverse_rms(widened) * gain[...]).astype(BF16)
 
     meta_copies = [
         remote(meta.at[2], meta.at[2 - step], meta_send.at[i], meta_recv.at[i], device(0, step))
@@ -578,7 +603,7 @@
 
     def input_grad(unit, saved, cotangent, target):
         sum_own(unit)
-        weighted = stage[...] * norm_gain[...]
+        weighted = stage[...] * gain[...]
         widened = saved.astype(F32)
         inverse = inverse_rms(widened)
         correction = jnp.mean(weighted * widened, axis=-1, keepdims=True)
@@ -598,37 +623,38 @@
             device_id_type=MESH,
         )
 
-    for batch, (ids, gates) in enumerate(
-        ((fwd_ids, fwd_gates), (bwd_ids, bwd_gates), (fwd_ids, fwd_gates), (bwd_ids, bwd_gates))
-    ):
+    need("fwd_ids", "fwd_gates", "bwd_ids", "bwd_gates")
+    for batch in range(4):
         begin = 2 * topk * batch
-        meta[2, :, begin : begin + topk] = ids[batch // 2, 0].astype(F32)
-        meta[2, :, begin + topk : begin + 2 * topk] = gates[batch // 2, 0]
+        meta[2, begin : begin + topk, :token_rows] = ids[batch % 2, batch // 2].astype(F32)
+        meta[2, begin + topk : begin + 2 * topk, :token_rows] = gates[batch % 2, batch // 2]
     current, cotangent = moved.at[0], moved.at[1]
-    forth = move(0, fwd_out.at[0], after)
+    forth = move(0, outs.at[0], after)
     upward = move(1, grads, before)
 
     def begin_spread(unit):
         if unit == 0:
-            held[0, 2] = normalize(fwd_state[0])
-            pl.semaphore_wait(barrier, chips + 2)
-            for copy in meta_copies:
-                copy.start()
+            need("fwd_state", "gain")
+            held[0, 2] = normalize(inputs[0])
         elif unit == 1:
-            held[1, 2] = normalize(saved_input[0, 0])
+            need("saved0", "gain")
+            held[1, 2] = normalize(inputs[2])
         elif unit == 2:
-            held[2, 2] = grad_state[0]
+            need("grad_state")
         elif unit == 3:
-            held[3, 2] = normalize(saved_input[1, 0])
+            need("saved1", "gain")
+            held[3, 2] = normalize(inputs[3])
         elif unit == 4:
+            need("new_tokens")
             forth.wait()
-            current[...] = jnp.where(pipe == 0, new_tokens[0], current[...])
+            current[...] = jnp.where(pipe == 0, inputs[1], current[...])
             held[4, 2] = normalize(current[...])
             release(0)
             sums_sent(0)
         else:
+            need("new_grads")
             upward.wait()
-            cotangent[...] = jnp.where(pipe == sections - 1, new_grads[0], cotangent[...])
+            cotangent[...] = jnp.where(pipe == sections - 1, inputs[4], cotangent[...])
             held[5, 2] = cotangent[...]
             release(2)
             sums_sent(1)
@@ -643,26 +669,35 @@
             for batch in range(4):
                 begin = 2 * topk * batch
                 weights = slot_weights(
-                    meta[slot, :, begin : begin + topk],
-                    meta[slot, :, begin + topk : begin + 2 * topk],
+                    meta[slot, begin : begin + topk, :token_rows],
+                    meta[slot, begin + topk : begin + 2 * topk, :token_rows],
                 )
-                table[batch, slot] = jnp.transpose(weights).reshape(chips, slots, token_rows)
-
-        for copy in weight_copies:
-            copy.wait()
+                table[batch, slot] = weights.reshape(chips, slots, token_rows)
+
+        need("gate", "up", "down")
+
+    finals = [
+        pltpu.make_async_copy(outs.at[i], target.at[0], output_sem.at[i])
+        for i, target in enumerate((fwd_out, grad_out))
+    ]
 
     def complete(unit):
         if unit == 0:
-            mixture(0, fwd_state.at[0], fwd_out.at[0])
+            mixture(0, inputs.at[0], outs.at[0])
             forth.start()
         elif unit == 1:
-            input_grad(1, saved_input[0, 0], grad_state.at[0], grads)
+            input_grad(1, inputs[2], held.at[2, 2], grads)
             upward.start()
         elif unit == 2:
-            mixture(2, current, fwd_out.at[0])
+            mixture(2, current, outs.at[0])
+            finals[0].start()
         else:
-            input_grad(3, saved_input[1, 0], cotangent, grad_out.at[0])
-
+            input_grad(3, inputs[3], cotangent, outs.at[1])
+            finals[1].start()
+
+    pl.semaphore_wait(barrier, chips + 2)
+    for copy in meta_copies:
+        copy.start()
     steps = {
         "spread": begin_spread,
         "tables": tables,
@@ -679,6 +714,8 @@
     }
     for name, *which in ORDER:
         steps[name](*which)
+    for copy in finals:
+        copy.wait()
 
     for copy in meta_copies:
         copy.wait_send()
@@ -696,27 +733,58 @@
                 copy.wait_send()
 
 
+def hand_over(first, second, first_out, second_out, held, in_sems, out_sems):
+    pairs = enumerate(((first, first_out), (second, second_out)))
+    arrive, leave = [], []
+    for i, (source, target) in pairs:
+        for half in range(PARTS):
+            size = held.shape[-1] // PARTS
+            cut = pl.ds(half * size, size)
+            between = held.at[i, :, :, cut]
+            arrive.append(
+                pltpu.make_async_copy(source.at[:, :, cut], between, in_sems.at[i, half])
+            )
+            leave.append(
+                pltpu.make_async_copy(between, target.at[:, :, cut], out_sems.at[i, half])
+            )
+    for copy in arrive:
+        copy.start()
+    for before, after in zip(arrive, leave):
+        before.wait()
+        after.start()
+    for copy in leave:
+        copy.wait()
+
+
 def shards(*arrays):
     fwd_state, fwd_ids, w_gate = arrays[0], arrays[9], arrays[6]
     token_rows, width = fwd_state.shape[1:]
     hidden = w_gate.shape[2]
     chips = lax.axis_size("expert") // 2
-    slots = token_rows * fwd_ids.shape[3] // chips
+    topk = fwd_ids.shape[3]
+    slots = token_rows * topk // chips
     count = 2 * chips * slots
     dma = pltpu.SemaphoreType.DMA
-    vmem = pl.BlockSpec(memory_space=pltpu.VMEM)
     hbm = pl.BlockSpec(memory_space=pl.ANY)
     row = jax.ShapeDtypeStruct(fwd_state.shape, BF16)
-    return pl.pallas_call(
+    routes = [jnp.transpose(array, (0, 1, 3, 2)) for array in arrays[9:]]
+    results = pl.pallas_call(
         kernel,
         out_shape=(row, row),
-        in_specs=[vmem] * 6 + [hbm] * 3 + [vmem] * 4,
-        out_specs=(vmem, vmem),
+        in_specs=[hbm] * len(arrays),
+        out_specs=(hbm, hbm),
         scratch_shapes=[
+            pltpu.VMEM((5, token_rows, width), BF16),
+            pltpu.VMEM((1, width), F32),
+            pltpu.VMEM((2, 2, topk, token_rows), jnp.int32),
+            pltpu.VMEM((2, 2, topk, token_rows), F32),
+            pltpu.VMEM((2, token_rows, width), BF16),
+            dma((14,)),
+            dma((2,)),
             pltpu.VMEM((width, hidden), BF16),
             pltpu.VMEM((width, hidden), BF16),
             pltpu.VMEM((hidden, width), BF16),
-            pltpu.VMEM((5, token_rows, 128), F32),
+            pltpu.VMEM((5, 8 * topk, 128), F32),
             pltpu.VMEM((4, 5, chips, slots, token_rows), F32),
             pltpu.VMEM((6, 5, token_rows, width), BF16),
             pltpu.VMEM((4, 5, slots, width), BF16),
@@ -739,7 +807,6 @@
             pltpu.VMEM((token_rows, width), F32),
             pltpu.VMEM((2, token_rows, width), BF16),
             pltpu.VMEM((token_rows, width), BF16),
-            dma((3,)),
             dma((4,)),
             dma((4,)),
             dma((6, PARTS, 13)),
@@ -757,7 +824,19 @@
             collective_id=0, has_side_effects=True, vmem_limit_bytes=60 * 2**20
         ),
         name="relay",
-    )(*arrays)
+    )(*arrays[:9], *routes)
+    return pl.pallas_call(
+        hand_over,
+        out_shape=(row, row),
+        in_specs=[hbm] * 2,
+        out_specs=(hbm, hbm),
+        scratch_shapes=[
+            pltpu.VMEM((2, *fwd_state.shape), BF16),
+            dma((2, PARTS)),
+            dma((2, PARTS)),
+        ],
+        name="hand_over",
+    )(*results)
 
 
 def solution(mesh):

time: 187 us -> 178 us (0.952)
  local copies, waits for them, and re-layouts: 8.82 us -> 0 us
    unnamed x6 -> x0, local copies, waits for them, and re-layouts: 8.82 us -> none
    pallas_call x1 -> x2, Pallas kernels: 178 us -> 177 us  [the longest x1 175 us: shards(): pl.pallas_call(kernel, out_shape=(row, row), in_specs=[hbm] * len(arrays)...]
where the time goes in v3:
time: 178 us
  Pallas kernels  177 us (99%)
    pallas_call x1, Pallas kernels, shards(): pl.pallas_call(kernel, out_shape=(row, row), in_specs=[hbm] * len(arrays)...  175 us

profile of v3, /device:TPU:1, one launch (start us, length us, event | category | flops | bytes accessed | tf_op | source)
XLA Modules:
  0.0 177.8 jit_solution(2412539993536654925)
XLA Ops:
  0.6 175.2 %relay.1 = (bf16[1,32,3584]{2,1,0:T(8,128)(2,1)}, bf16[1,32,3584]{2,1,0:T(8,128)(2,1)}) custom-call(bf16[1,32,3584]{2,1,0:T(8,128)(2,1)} %fwd_state.1, bf16[1,32,3584]{2,1,0:T(8,128)(2,1)} %new_tokens.1, bf16[2,1,32,3584]{3,2,1,0:T(8,128)(2,1)} %saved_input.1, bf16[1,32,3584]{2,1,0:T(8,128)(2,1)} %grad_state.1, bf16[1,32,3584]{2,1,0:T(8,128)(2,1)} %new_grads.1, ...), custom_call_target="tpu_custom_call" | custom-call | tf_op jit(solution)/shard_map/relay/pallas_call | solution.py:771
  175.8 1.8 %hand_over.1 = (bf16[1,32,3584]{2,1,0:T(8,128)(2,1)}, bf16[1,32,3584]{2,1,0:T(8,128)(2,1)}) custom-call(bf16[1,32,3584]{2,1,0:T(8,128)(2,1)} %get-tuple-element.4.first, bf16[1,32,3584]{2,1,0:T(8,128)(2,1)} %get-tuple-element.5.second), custom_call_target="tpu_custom_call" | custom-call | tf_op jit(solution)/shard_map/hand_over/pallas_call | solution.py:828

commit v4 on v3

--- a/solution.py
+++ b/solution.py
@@ -27,82 +27,84 @@
 
 ORDER = (
     ("spread", 2),
-    ("spread", 1),
     ("spread", 0),
     ("tables", 0),
+    ("spread", 1),
+    ("relay", 0, 1),
+    ("relay", 0, 0),
+    ("relay", 1, 0),
+    ("finish", 0, 1),
+    ("finish", 0, 0),
+    ("relay", 1, 1),
+    ("relay", 2, 1),
     ("relay", 2, 0),
-    ("relay", 2, 1),
-    ("relay", 1, 0),
-    ("relay", 1, 1),
-    ("finish", 2, 0),
     ("finish", 1, 0),
-    ("finish", 1, 1),
-    ("finish", 2, 1),
-    ("relay", 0, 0),
-    ("relay", 0, 1),
-    ("spread", 3),
-    ("collect", 2, 0),
-    ("collect", 1, 0),
-    ("collect", 1, 1),
-    ("recompute", 1),
-    ("collect", 2, 1),
-    ("finish", 0, 0),
-    ("finish", 0, 1),
-    ("backward", 1),
-    ("relay", 3, 0),
-    ("back", 1, 0),
-    ("back", 1, 1),
     ("collect", 0, 0),
     ("collect", 0, 1),
+    ("finish", 1, 1),
+    ("forward", 0),
+    ("finish", 2, 0),
+    ("collect", 1, 0),
+    ("finish", 2, 1),
+    ("back", 0, 0),
+    ("collect", 2, 0),
+    ("collect", 1, 1),
+    ("back", 0, 1),
+    ("spread", 3),
+    ("collect", 2, 1),
+    ("recompute", 1),
+    ("far", 0, 0),
+    ("backward", 1),
+    ("far", 0, 1),
+    ("back", 1, 1),
+    ("near", 0, 0),
+    ("back", 1, 0),
+    ("near", 0, 1),
+    ("far", 1, 1),
+    ("far", 1, 0),
+    ("own", 0),
+    ("relay", 3, 0),
+    ("near", 1, 1),
+    ("near", 1, 0),
+    ("relay", 3, 1),
+    ("spread", 4),
+    ("own", 1),
     ("finish", 3, 0),
-    ("forward", 0),
-    ("far", 1, 0),
-    ("back", 0, 1),
-    ("far", 1, 1),
-    ("back", 0, 0),
+    ("relay", 4, 0),
+    ("relay", 4, 1),
+    ("spread", 5),
+    ("finish", 4, 1),
+    ("finish", 4, 0),
+    ("relay", 5, 1),
+    ("collect", 4, 1),
     ("collect", 3, 0),
-    ("near", 1, 0),
-    ("near", 1, 1),
-    ("far", 0, 1),
-    ("far", 0, 0),
-    ("own", 1),
-    ("relay", 3, 1),
-    ("near", 0, 1),
-    ("near", 0, 0),
-    ("spread", 5),
+    ("relay", 5, 0),
     ("finish", 3, 1),
-    ("own", 0),
-    ("relay", 5, 0),
-    ("relay", 5, 1),
-    ("spread", 4),
+    ("collect", 4, 0),
+    ("finish", 5, 1),
+    ("forward", 2),
     ("finish", 5, 0),
-    ("relay", 4, 0),
-    ("finish", 5, 1),
+    ("back", 2, 0),
     ("collect", 3, 1),
+    ("collect", 5, 1),
     ("recompute", 3),
-    ("relay", 4, 1),
+    ("back", 2, 1),
     ("collect", 5, 0),
-    ("finish", 4, 0),
-    ("collect", 5, 1),
-    ("finish", 4, 1),
+    ("settle", 0),
+    ("far", 2, 0),
     ("backward", 3),
+    ("far", 2, 1),
     ("back", 3, 0),
-    ("collect", 4, 1),
-    ("collect", 4, 0),
     ("back", 3, 1),
-    ("forward", 2),
+    ("settle", 1),
+    ("near", 2, 1),
     ("far", 3, 0),
-    ("back", 2, 0),
-    ("back", 2, 1),
+    ("far", 3, 1),
+    ("near", 2, 0),
     ("near", 3, 0),
-    ("far", 3, 1),
-    ("far", 2, 0),
-    ("far", 2, 1),
     ("near", 3, 1),
-    ("near", 2, 0),
-    ("near", 2, 1),
+    ("own", 2),
     ("own", 3),
-    ("own", 2),
 )
 
 
@@ -184,7 +186,7 @@
     slots = recv.shape[4]
     count = chips * slots
     hidden = gate_w.shape[1]
-    wide = 256
+    wide = 256 if width // PARTS % 256 == 0 else width // PARTS
     after = lax.rem(pipe + 1, sections)
     before = lax.rem(pipe + sections - 1, sections)
 
@@ -380,12 +382,14 @@
         crossing = cross_copies(unit, half)
         for i, (slot, steps) in enumerate(FAR_STEPS):
             arrivals[i].wait_recv()
-            targets = near(unit, slot) + [
+            targets = [
                 (expert(*at), far.at[LOTS[unit], 3 * i + n]) for n, at in enumerate(steps)
             ]
             pick(unit, half, slot, 1, targets)
             for n in range(3):
                 beyond[3 * i + n].start()
+        for i, slot in enumerate((0, 4)):
+            pick(unit, half, slot, 1, near(unit, slot))
             crossing[1 + i].start()
 
     def release(unit):
@@ -432,31 +436,35 @@
         )
 
     def result_copies(unit, half):
-        crossing = remote(
-            results.at[unit, 1, pl.ds(0, 5), :, part(half)],
-            cross_in.at[unit, :, :, part(half)],
-            back_ssem.at[unit, half, 0],
-            back_rsem.at[unit, half, 0],
-            device(1, 0),
-        )
-        return [crossing] + [
+        straight = [
             remote(
                 results.at[unit, to, slot, :, part(half)],
                 far_in.at[unit, i, :, part(half)],
-                back_ssem.at[unit, half, 1 + i],
-                back_rsem.at[unit, half, 1 + i],
+                back_ssem.at[unit, half, i],
+                back_rsem.at[unit, half, i],
                 device(across, -step),
             )
             for i, (to, slot, across, step) in enumerate(FAR_ROWS)
         ]
+        crossing = [
+            remote(
+                results.at[unit, 1, slots_of, :, part(half)],
+                cross_in.at[unit, slots_of, :, part(half)],
+                back_ssem.at[unit, half, 6 + i],
+                back_rsem.at[unit, half, 6 + i],
+                device(1, 0),
+            )
+            for i, slots_of in enumerate((pl.ds(0, 1), pl.ds(4, 1), pl.ds(1, 3)))
+        ]
+        return straight + crossing
 
     def sum_copies(unit, half, hop):
         return [
             remote(
                 sums_out.at[unit % 2, hop, i, :, part(half)],
                 sums_in.at[unit, hop, i, :, part(half)],
-                back_ssem.at[unit, half, 7 + 2 * hop + i],
-                back_rsem.at[unit, half, 7 + 2 * hop + i],
+                back_ssem.at[unit, half, 9 + 2 * hop + i],
+                back_rsem.at[unit, half, 9 + 2 * hop + i],
                 device(0, step),
             )
             for i, step in enumerate((-1, 1))
@@ -493,7 +501,7 @@
 
     def sum_far(unit, half):
         onward = sum_copies(unit, half, 0)
-        for copy in result_copies(unit, half):
+        for copy in result_copies(unit, half)[:8]:
             copy.wait_recv()
         for i, (slot, steps) in enumerate(FAR_STEPS):
             terms = close_terms(unit, slot) + [
@@ -509,6 +517,7 @@
 
     def sum_near(unit, half):
         arrivals, onward = sum_copies(unit, half, 0), sum_copies(unit, half, 1)
+        result_copies(unit, half)[8].wait_recv()
         for i, slot in enumerate((1, 3)):
             arrivals[i].wait_recv()
             target = sums_out.at[unit % 2, 1, i]
@@ -602,10 +611,10 @@
         target[...] = (base[...].astype(F32) + stage[...]).astype(BF16)
 
     def input_grad(unit, saved, cotangent, target):
+        inverse = inverse_rms(saved.astype(F32))
         sum_own(unit)
         weighted = stage[...] * gain[...]
         widened = saved.astype(F32)
-        inverse = inverse_rms(widened)
         correction = jnp.mean(weighted * widened, axis=-1, keepdims=True)
         target[...] = (
             cotangent[...].astype(F32)
@@ -698,7 +707,37 @@
     pl.semaphore_wait(barrier, chips + 2)
     for copy in meta_copies:
         copy.start()
+    def hops_sent(unit):
+        for half in range(PARTS):
+            for copy in first_hop(unit, half) + second_hop(unit, half):
+                copy.wait_send()
+
+    def results_sent(unit):
+        for half in range(PARTS):
+            for copy in result_copies(unit, half):
+                copy.wait_send()
+
+    def settle(stage):
+        if stage == 0:
+            for copy in meta_copies:
+                copy.wait_send()
+            for unit in range(4):
+                hops_sent(unit)
+            for unit in (1, 3):
+                release(unit)
+            for unit in (0, 1):
+                results_sent(unit)
+        elif stage == 1:
+            for unit in (4, 5):
+                hops_sent(unit)
+                release(unit)
+        else:
+            for unit in (2, 3):
+                results_sent(unit)
+                sums_sent(unit)
+
     steps = {
+        "settle": settle,
         "spread": begin_spread,
         "tables": tables,
         "relay": relay,
@@ -714,23 +753,9 @@
     }
     for name, *which in ORDER:
         steps[name](*which)
+    settle(2)
     for copy in finals:
         copy.wait()
-
-    for copy in meta_copies:
-        copy.wait_send()
-    for unit in range(6):
-        for half in range(PARTS):
-            for copy in first_hop(unit, half) + second_hop(unit, half):
-                copy.wait_send()
-    for unit in (4, 1, 5, 3):
-        release(unit)
-    for unit in (2, 3):
-        sums_sent(unit)
-    for unit in range(4):
-        for half in range(PARTS):
-            for copy in result_copies(unit, half):
-                copy.wait_send()
 
 
 def hand_over(first, second, first_out, second_out, held, in_sems, out_sems):
@@ -815,8 +840,8 @@
             dma((6, PARTS)),
             dma((4, PARTS)),
             dma((4, PARTS)),
-            dma((4, PARTS, 11)),
-            dma((4, PARTS, 11)),
+            dma((4, PARTS, 13)),
+            dma((4, PARTS, 13)),
             dma((2,)),
             dma((2,)),
         ],

time: 178 us -> 175 us (0.983)
  Pallas kernels: 177 us -> 173 us
    pallas_call x1, Pallas kernels: 175 us -> 171 us  [shards(): pl.pallas_call(kernel, out_shape=(row, row), in_specs=[hbm] * len(arrays)...]
where the time goes in v4:
time: 175 us; the launch traced here: 174 us
  Pallas kernels  173 us (99%)
    pallas_call x1, Pallas kernels, shards(): pl.pallas_call(kernel, out_shape=(row, row), in_specs=[hbm] * len(arrays)...  171 us

profile of v4, /device:TPU:1, one launch (start us, length us, event | category | flops | bytes accessed | tf_op | source)
XLA Modules:
  0.0 174.1 jit_solution(456874295307150987)
XLA Ops:
  0.6 171.5 %relay.1 = (bf16[1,32,3584]{2,1,0:T(8,128)(2,1)}, bf16[1,32,3584]{2,1,0:T(8,128)(2,1)}) custom-call(bf16[1,32,3584]{2,1,0:T(8,128)(2,1)} %fwd_state.1, bf16[1,32,3584]{2,1,0:T(8,128)(2,1)} %new_tokens.1, bf16[2,1,32,3584]{3,2,1,0:T(8,128)(2,1)} %saved_input.1, bf16[1,32,3584]{2,1,0:T(8,128)(2,1)} %grad_state.1, bf16[1,32,3584]{2,1,0:T(8,128)(2,1)} %new_grads.1, ...), custom_call_target="tpu_custom_call" | custom-call | tf_op jit(solution)/shard_map/relay/pallas_call | solution.py:796
  172.1 1.8 %hand_over.1 = (bf16[1,32,3584]{2,1,0:T(8,128)(2,1)}, bf16[1,32,3584]{2,1,0:T(8,128)(2,1)}) custom-call(bf16[1,32,3584]{2,1,0:T(8,128)(2,1)} %get-tuple-element.4.first, bf16[1,32,3584]{2,1,0:T(8,128)(2,1)} %get-tuple-element.5.second), custom_call_target="tpu_custom_call" | custom-call | tf_op jit(solution)/shard_map/hand_over/pallas_call | solution.py:853

commit v5 on v4

--- a/solution.py
+++ b/solution.py
@@ -634,9 +634,9 @@
 
     need("fwd_ids", "fwd_gates", "bwd_ids", "bwd_gates")
     for batch in range(4):
-        begin = 2 * topk * batch
-        meta[2, begin : begin + topk, :token_rows] = ids[batch % 2, batch // 2].astype(F32)
-        meta[2, begin + topk : begin + 2 * topk, :token_rows] = gates[batch % 2, batch // 2]
+        begin = token_rows * batch
+        meta[2, :topk, begin : begin + token_rows] = ids[batch % 2, batch // 2].astype(F32)
+        meta[2, topk:, begin : begin + token_rows] = gates[batch % 2, batch // 2]
     current, cotangent = moved.at[0], moved.at[1]
     forth = move(0, outs.at[0], after)
     upward = move(1, grads, before)
@@ -676,10 +676,10 @@
         @pl.loop(0, 5)
         def _(slot):
             for batch in range(4):
-                begin = 2 * topk * batch
+                begin = token_rows * batch
                 weights = slot_weights(
-                    meta[slot, begin : begin + topk, :token_rows],
-                    meta[slot, begin + topk : begin + 2 * topk, :token_rows],
+                    meta[slot, :topk, begin : begin + token_rows],
+                    meta[slot, topk:, begin : begin + token_rows],
                 )
                 table[batch, slot] = weights.reshape(chips, slots, token_rows)
 
@@ -809,7 +809,7 @@
             pltpu.VMEM((width, hidden), BF16),
             pltpu.VMEM((width, hidden), BF16),
             pltpu.VMEM((hidden, width), BF16),
-            pltpu.VMEM((5, 8 * topk, 128), F32),
+            pltpu.VMEM((5, 2 * topk, 4 * token_rows), F32),
             pltpu.VMEM((4, 5, chips, slots, token_rows), F32),
             pltpu.VMEM((6, 5, token_rows, width), BF16),
             pltpu.VMEM((4, 5, slots, width), BF16),

time: 175 us -> 174 us (level)
  no operation moved by 1% of the time
where the time goes in v5:
time: 174 us; the launch traced here: 173 us
  Pallas kernels  172 us (99%)
    pallas_call x1, Pallas kernels, shards(): pl.pallas_call(kernel, out_shape=(row, row), in_specs=[hbm] * len(arrays)...  170 us

profile of v5, /device:TPU:1, one launch (start us, length us, event | category | flops | bytes accessed | tf_op | source)
XLA Modules:
  0.0 172.6 jit_solution(17486294965077346173)
XLA Ops:
  0.6 170.0 %relay.1 = (bf16[1,32,3584]{2,1,0:T(8,128)(2,1)}, bf16[1,32,3584]{2,1,0:T(8,128)(2,1)}) custom-call(bf16[1,32,3584]{2,1,0:T(8,128)(2,1)} %fwd_state.1, bf16[1,32,3584]{2,1,0:T(8,128)(2,1)} %new_tokens.1, bf16[2,1,32,3584]{3,2,1,0:T(8,128)(2,1)} %saved_input.1, bf16[1,32,3584]{2,1,0:T(8,128)(2,1)} %grad_state.1, bf16[1,32,3584]{2,1,0:T(8,128)(2,1)} %new_grads.1, ...), custom_call_target="tpu_custom_call" | custom-call | tf_op jit(solution)/shard_map/relay/pallas_call | solution.py:796
  170.6 1.8 %hand_over.1 = (bf16[1,32,3584]{2,1,0:T(8,128)(2,1)}, bf16[1,32,3584]{2,1,0:T(8,128)(2,1)}) custom-call(bf16[1,32,3584]{2,1,0:T(8,128)(2,1)} %get-tuple-element.4.first, bf16[1,32,3584]{2,1,0:T(8,128)(2,1)} %get-tuple-element.5.second), custom_call_target="tpu_custom_call" | custom-call | tf_op jit(solution)/shard_map/hand_over/pallas_call | solution.py:853
